TPU v7x, 256 devices: a whole 4x4x8 slice. The times are simulated.
256 devices in a mesh: cells: 32 (over z, x), genes: 8 (over y, core).
Axes of the slice: x: 4, y: 4, z: 8, core: 2. Of those that a mesh axis runs over, the one named last changes fastest.
Arguments:
- block_tiles: bfloat16 [10240, 1024, 128], P('cells', 'genes'), may hold values from -0.375 to 0.375
- block_coords: int32 [10240, 16], P('cells', 'genes'), may hold values from 0 to 31, as said below
- block_counts: int32 [32, 8], P('cells', 'genes'), may hold values from 40 to 320, as said below
- basis_rows: bfloat16 [32768, 256], P(('cells', 'genes')), may hold values from -0.03125 to 0.03125
Outputs:
- gene_products: float32 [32768, 256], P(('cells', 'genes'))
Inputs may be any that keep to these rules, and one draw needn't show every extreme that they name: `block_coords`: column 2 g of device rows gives a block of cells below 16, column 2 g + 1 a tile of genes below 32; the live slots of one device name distinct pairs; slots at or past the device's count hold valid coordinates and tiles that are not part of X. `block_counts`: at least 40 live slots a device; some device uses all 320.
All inputs are finite; a program needn't handle non-finite values.
Results may differ from a plain program's by a relative error of at most 0.0017.
Values may be sent and summed in bfloat16 or wider, within the bound.
A program may use at most 64 MiB of HBM per device.

v0:
```python
import jax
import jax.numpy as jnp
from jax import lax
from jax.sharding import PartitionSpec as P

BLK = 128
ROWS_C = 2048
SLOTS_PER_RB = 20


def drop_dead(product, first_slot, group_size, live_count):
    live = first_slot + jnp.arange(group_size) < live_count
    return jnp.where(live[:, None, None], product, jnp.zeros_like(product))


def local(block_tiles, block_coords, block_counts, basis_rows):
    slot_total = block_tiles.shape[0]
    tile_edge = block_tiles.shape[2]
    rank_width = basis_rows.shape[1]
    gathered = lax.all_gather(basis_rows, "cells", axis=0, tiled=True)
    group_blocks = gathered.shape[0] // tile_edge
    basis_blocks = gathered.reshape(group_blocks, tile_edge, rank_width)
    row_count = ROWS_C // BLK
    group_size = 2 * SLOTS_PER_RB
    live_count = block_counts[0, 0]
    row_index = block_coords[:, 0]
    gene_index = block_coords[:, 1]
    turns = slot_total // group_size

    def cell_turn(turn_index, running):
        first_slot = turn_index * group_size
        piece = lax.dynamic_slice_in_dim(block_tiles, first_slot, group_size, 0)
        rows_here = lax.dynamic_slice_in_dim(row_index, first_slot, group_size, 0)
        genes_here = lax.dynamic_slice_in_dim(gene_index, first_slot, group_size, 0)
        chosen = basis_blocks[genes_here]
        product = jnp.einsum("sab,sbk->sak", piece, chosen, preferred_element_type=jnp.float32)
        product = drop_dead(product, first_slot, group_size, live_count)
        return running.at[rows_here].add(product)

    row_sums = lax.fori_loop(
        0, turns, cell_turn, jnp.zeros((row_count, tile_edge, rank_width), jnp.float32)
    )
    row_flat = row_sums.reshape(row_count * tile_edge, rank_width)
    cell_basis = lax.psum(row_flat, "genes").astype(jnp.bfloat16)
    basis_cells = cell_basis.reshape(row_count, tile_edge, rank_width)

    def gene_turn(turn_index, running):
        first_slot = turn_index * group_size
        piece = lax.dynamic_slice_in_dim(block_tiles, first_slot, group_size, 0)
        rows_here = lax.dynamic_slice_in_dim(row_index, first_slot, group_size, 0)
        genes_here = lax.dynamic_slice_in_dim(gene_index, first_slot, group_size, 0)
        chosen = basis_cells[rows_here]
        product = jnp.einsum("sab,sak->sbk", piece, chosen, preferred_element_type=jnp.float32)
        product = drop_dead(product, first_slot, group_size, live_count)
        return running.at[genes_here].add(product)

    gene_sums = lax.fori_loop(
        0, turns, gene_turn, jnp.zeros((group_blocks, tile_edge, rank_width), jnp.float32)
    )
    gene_flat = gene_sums.reshape(group_blocks * tile_edge, rank_width)
    return lax.psum_scatter(gene_flat, "cells", scatter_dimension=0, tiled=True)


def solution(mesh):
    return jax.shard_map(
        local,
        mesh=mesh,
        in_specs=(
            P("cells", "genes", None),
            P("cells", "genes"),
            P("cells", "genes"),
            P(("cells", "genes"), None),
        ),
        out_specs=P(("cells", "genes"), None),
        check_vma=False,
    )
```

profile of v0, /device:TPU:8, one launch (start us, length us, event | category | flops | bytes accessed | tf_op | source)
XLA Modules:
  0.0 695.2 jit_solution(17048328373035769528)
XLA Ops:
  6.5 0.7 all-gather.2.cloned.1.call-update
  7.3 0.8 slice_reduce_fusion
  8.1 82.6 %all-gather.2.cloned.1.call-done = bf16[4096,256]{1,0:T(8,128)(2,1)} async-done(((bf16[128,256]{1,0:T(8,128)(2,1)}), bf16[4096,256]{1,0:T(8,128)(2,1)}) %all-gather.2.cloned.1.call-update) | async-done | bytes 2097168 | tf_op jit(solution)/shard_map/all_gather | solution.py:20
  90.9 152.8 %while.26 = (s32[]{:T(128)}, f32[16,128,256]{2,1,0:T(8,128)S(1)}, s32[320]{0:T(512)S(1)}, s32[]{:T(128)}, bf16[320,128,128]{2,1,0:T(8,128)(2,1)}, /*index=5*/s32...) while((s32[]{:T(128)}, f32[16,128,256]{2,1,0:T(8,128)S(1)}, ...), condition=%wide.region_2.3_spmd, body=%wide.region_0.2_spmd.sunk | while | flops 338167104 | bytes 30152028 | solution.py:40
  90.9 0.7 add_compare_fusion.4
  91.7 4.0 gather_fusion
  95.7 5.3 broadcast_select_fusion.4
  100.9 9.1 %scatter_fusion = f32[16,128,256]{2,1,0:T(8,128)S(1)} fusion(f32[16,128,256]{2,1,0:T(8,128)S(1)} %get-tuple-element.402, s32[40]{0:T(128)S(1)} %get-tuple-element.379, f32[40,128,256]{2,1,0:T(8,128)} %broadcast_select_fusion.4), kind=kCustom, calls=%fused_computation.2.clone.1 | custom fusion | flops 1310720 | bytes 15728800 | tf_op jit(solution)/shard_map/while/body/eval_jaxpr/scatter-add | solution.py:38
  110.0 0.7 add_compare_fusion.4
  110.8 4.0 gather_fusion
  114.8 5.3 broadcast_select_fusion.4
  120.0 9.1 %scatter_fusion = f32[16,128,256]{2,1,0:T(8,128)S(1)} fusion(f32[16,128,256]{2,1,0:T(8,128)S(1)} %get-tuple-element.402, s32[40]{0:T(128)S(1)} %get-tuple-element.379, f32[40,128,256]{2,1,0:T(8,128)} %broadcast_select_fusion.4), kind=kCustom, calls=%fused_computation.2.clone.1 | custom fusion | flops 1310720 | bytes 15728800 | tf_op jit(solution)/shard_map/while/body/eval_jaxpr/scatter-add | solution.py:38
  129.1 0.7 add_compare_fusion.4
  129.9 4.0 gather_fusion
  133.9 5.3 broadcast_select_fusion.4
  139.1 9.1 %scatter_fusion = f32[16,128,256]{2,1,0:T(8,128)S(1)} fusion(f32[16,128,256]{2,1,0:T(8,128)S(1)} %get-tuple-element.402, s32[40]{0:T(128)S(1)} %get-tuple-element.379, f32[40,128,256]{2,1,0:T(8,128)} %broadcast_select_fusion.4), kind=kCustom, calls=%fused_computation.2.clone.1 | custom fusion | flops 1310720 | bytes 15728800 | tf_op jit(solution)/shard_map/while/body/eval_jaxpr/scatter-add | solution.py:38
  148.2 0.7 add_compare_fusion.4
  149.0 4.0 gather_fusion
  153.0 5.3 broadcast_select_fusion.4
  158.2 9.1 %scatter_fusion = f32[16,128,256]{2,1,0:T(8,128)S(1)} fusion(f32[16,128,256]{2,1,0:T(8,128)S(1)} %get-tuple-element.402, s32[40]{0:T(128)S(1)} %get-tuple-element.379, f32[40,128,256]{2,1,0:T(8,128)} %broadcast_select_fusion.4), kind=kCustom, calls=%fused_computation.2.clone.1 | custom fusion | flops 1310720 | bytes 15728800 | tf_op jit(solution)/shard_map/while/body/eval_jaxpr/scatter-add | solution.py:38
  167.3 0.7 add_compare_fusion.4
  168.1 4.0 gather_fusion
  172.1 5.3 broadcast_select_fusion.4
  177.4 9.1 %scatter_fusion = f32[16,128,256]{2,1,0:T(8,128)S(1)} fusion(f32[16,128,256]{2,1,0:T(8,128)S(1)} %get-tuple-element.402, s32[40]{0:T(128)S(1)} %get-tuple-element.379, f32[40,128,256]{2,1,0:T(8,128)} %broadcast_select_fusion.4), kind=kCustom, calls=%fused_computation.2.clone.1 | custom fusion | flops 1310720 | bytes 15728800 | tf_op jit(solution)/shard_map/while/body/eval_jaxpr/scatter-add | solution.py:38
  186.4 0.7 add_compare_fusion.4
  187.2 4.0 gather_fusion
  191.2 5.3 broadcast_select_fusion.4
  196.4 9.1 %scatter_fusion = f32[16,128,256]{2,1,0:T(8,128)S(1)} fusion(f32[16,128,256]{2,1,0:T(8,128)S(1)} %get-tuple-element.402, s32[40]{0:T(128)S(1)} %get-tuple-element.379, f32[40,128,256]{2,1,0:T(8,128)} %broadcast_select_fusion.4), kind=kCustom, calls=%fused_computation.2.clone.1 | custom fusion | flops 1310720 | bytes 15728800 | tf_op jit(solution)/shard_map/while/body/eval_jaxpr/scatter-add | solution.py:38
  205.5 0.7 add_compare_fusion.4
  206.3 4.0 gather_fusion
  210.2 5.3 broadcast_select_fusion.4
  215.5 9.1 %scatter_fusion = f32[16,128,256]{2,1,0:T(8,128)S(1)} fusion(f32[16,128,256]{2,1,0:T(8,128)S(1)} %get-tuple-element.402, s32[40]{0:T(128)S(1)} %get-tuple-element.379, f32[40,128,256]{2,1,0:T(8,128)} %broadcast_select_fusion.4), kind=kCustom, calls=%fused_computation.2.clone.1 | custom fusion | flops 1310720 | bytes 15728800 | tf_op jit(solution)/shard_map/while/body/eval_jaxpr/scatter-add | solution.py:38
  224.6 0.7 add_compare_fusion.4
  225.4 4.0 gather_fusion
  229.3 5.3 broadcast_select_fusion.4
  234.6 9.1 %scatter_fusion = f32[16,128,256]{2,1,0:T(8,128)S(1)} fusion(f32[16,128,256]{2,1,0:T(8,128)S(1)} %get-tuple-element.402, s32[40]{0:T(128)S(1)} %get-tuple-element.379, f32[40,128,256]{2,1,0:T(8,128)} %broadcast_select_fusion.4), kind=kCustom, calls=%fused_computation.2.clone.1 | custom fusion | flops 1310720 | bytes 15728800 | tf_op jit(solution)/shard_map/while/body/eval_jaxpr/scatter-add | solution.py:38
  243.7 48.9 %all-reduce.1 = bf16[2048,256]{1,0:T(8,128)(2,1)} all-reduce(f32[2048,256]{1,0:T(8,128)S(1)} %bitcast.11), channel_id=1, replica_groups=mesh['cells'=32,'genes'=8] {'genes'}, use_global_device_ids=true, to_apply=%region_3.4 | all-reduce | flops 524288 | bytes 3145728 | tf_op jit(solution)/shard_map/psum | solution.py:44
  292.7 2.5 broadcast_in_dim.73
  295.2 170.9 %while.27 = (s32[]{:T(128)}, f32[32,128,256]{2,1,0:T(8,128)}, s32[320]{0:T(512)S(1)}, s32[]{:T(128)}, bf16[320,128,128]{2,1,0:T(8,128)(2,1)}, /*index=5*/s32[320...) while((s32[]{:T(128)}, f32[32,128,256]{2,1,0:T(8,128)}, ...), condition=%wide.region_6.7_spmd, body=%wide.region_4.6_spmd.sunk | while | flops 338167104 | bytes 30152028 | solution.py:57
  295.9 1.9 gather_fusion.1
  297.9 4.6 broadcast_select_fusion.5
  302.5 14.0 %scatter_fusion.1 = f32[32,128,256]{2,1,0:T(8,128)} fusion(f32[32,128,256]{2,1,0:T(8,128)} %get-tuple-element.435, s32[40]{0:T(128)S(1)} %get-tuple-element.388, f32[40,128,256]{2,1,0:T(8,128)} %broadcast_select_fusion.5), kind=kCustom, calls=%fused_computation.3.clone.1 | custom fusion | flops 1310720 | bytes 15728800 | tf_op jit(solution)/shard_map/while/body/eval_jaxpr/scatter-add | solution.py:55
  317.3 1.9 gather_fusion.1
  319.2 4.6 broadcast_select_fusion.5
  323.9 14.0 %scatter_fusion.1 = f32[32,128,256]{2,1,0:T(8,128)} fusion(f32[32,128,256]{2,1,0:T(8,128)} %get-tuple-element.435, s32[40]{0:T(128)S(1)} %get-tuple-element.388, f32[40,128,256]{2,1,0:T(8,128)} %broadcast_select_fusion.5), kind=kCustom, calls=%fused_computation.3.clone.1 | custom fusion | flops 1310720 | bytes 15728800 | tf_op jit(solution)/shard_map/while/body/eval_jaxpr/scatter-add | solution.py:55
  338.6 1.9 gather_fusion.1
  340.5 4.6 broadcast_select_fusion.5
  345.2 14.0 %scatter_fusion.1 = f32[32,128,256]{2,1,0:T(8,128)} fusion(f32[32,128,256]{2,1,0:T(8,128)} %get-tuple-element.435, s32[40]{0:T(128)S(1)} %get-tuple-element.388, f32[40,128,256]{2,1,0:T(8,128)} %broadcast_select_fusion.5), kind=kCustom, calls=%fused_computation.3.clone.1 | custom fusion | flops 1310720 | bytes 15728800 | tf_op jit(solution)/shard_map/while/body/eval_jaxpr/scatter-add | solution.py:55
  360.0 1.9 gather_fusion.1
  361.9 4.6 broadcast_select_fusion.5
  366.5 14.0 %scatter_fusion.1 = f32[32,128,256]{2,1,0:T(8,128)} fusion(f32[32,128,256]{2,1,0:T(8,128)} %get-tuple-element.435, s32[40]{0:T(128)S(1)} %get-tuple-element.388, f32[40,128,256]{2,1,0:T(8,128)} %broadcast_select_fusion.5), kind=kCustom, calls=%fused_computation.3.clone.1 | custom fusion | flops 1310720 | bytes 15728800 | tf_op jit(solution)/shard_map/while/body/eval_jaxpr/scatter-add | solution.py:55
  381.3 1.9 gather_fusion.1
  383.2 4.6 broadcast_select_fusion.5
  387.9 14.0 %scatter_fusion.1 = f32[32,128,256]{2,1,0:T(8,128)} fusion(f32[32,128,256]{2,1,0:T(8,128)} %get-tuple-element.435, s32[40]{0:T(128)S(1)} %get-tuple-element.388, f32[40,128,256]{2,1,0:T(8,128)} %broadcast_select_fusion.5), kind=kCustom, calls=%fused_computation.3.clone.1 | custom fusion | flops 1310720 | bytes 15728800 | tf_op jit(solution)/shard_map/while/body/eval_jaxpr/scatter-add | solution.py:55
  402.6 1.9 gather_fusion.1
  404.6 4.6 broadcast_select_fusion.5
  409.2 14.3 %scatter_fusion.1 = f32[32,128,256]{2,1,0:T(8,128)} fusion(f32[32,128,256]{2,1,0:T(8,128)} %get-tuple-element.435, s32[40]{0:T(128)S(1)} %get-tuple-element.388, f32[40,128,256]{2,1,0:T(8,128)} %broadcast_select_fusion.5), kind=kCustom, calls=%fused_computation.3.clone.1 | custom fusion | flops 1310720 | bytes 15728800 | tf_op jit(solution)/shard_map/while/body/eval_jaxpr/scatter-add | solution.py:55
  424.2 1.9 gather_fusion.1
  426.1 4.6 broadcast_select_fusion.5
  430.8 13.9 %scatter_fusion.1 = f32[32,128,256]{2,1,0:T(8,128)} fusion(f32[32,128,256]{2,1,0:T(8,128)} %get-tuple-element.435, s32[40]{0:T(128)S(1)} %get-tuple-element.388, f32[40,128,256]{2,1,0:T(8,128)} %broadcast_select_fusion.5), kind=kCustom, calls=%fused_computation.3.clone.1 | custom fusion | flops 1310720 | bytes 15728800 | tf_op jit(solution)/shard_map/while/body/eval_jaxpr/scatter-add | solution.py:55
  445.4 1.9 gather_fusion.1
  447.4 4.6 broadcast_select_fusion.5
  452.0 14.0 %scatter_fusion.1 = f32[32,128,256]{2,1,0:T(8,128)} fusion(f32[32,128,256]{2,1,0:T(8,128)} %get-tuple-element.435, s32[40]{0:T(128)S(1)} %get-tuple-element.388, f32[40,128,256]{2,1,0:T(8,128)} %broadcast_select_fusion.5), kind=kCustom, calls=%fused_computation.3.clone.1 | custom fusion | flops 1310720 | bytes 15728800 | tf_op jit(solution)/shard_map/while/body/eval_jaxpr/scatter-add | solution.py:55
  466.0 222.3 %reduce-scatter.2.cloned.1.call-done = f32[128,256]{1,0:T(8,128)} async-done(((f32[4096,256]{1,0:T(8,128)}), f32[128,256]{1,0:T(8,128)}) %reduce-scatter.2.cloned.1.call-update) | async-done | bytes 131088 | tf_op jit(solution)/shard_map/reduce_scatter | solution.py:61
  (44 shorter events, 6.9 us)
Async XLA Ops:
  6.5 84.2 %all-gather.2.cloned.1.call-start = ((), (), s32[]{:S(2)}) async-start(), calls=%async_computation.1 | async-start | bytes 2162688 | tf_op jit(solution)/shard_map/all_gather | solution.py:20
  7.3 681.1 %reduce-scatter.2.cloned.1.call-start = ((), (), s32[]{:S(2)}) async-start(), calls=%async_computation.2 | async-start | bytes 4325376 | tf_op jit(solution)/shard_map/reduce_scatter | solution.py:61
Sparse Core Ops, SparseCore 0:
  9.9 80.7 all-gather.1
  466.2 222.1 reduce-scatter.1
where the time goes:
time: 697 us; the launch traced here: 695 us
  waiting for transfers between devices  306 us (44%)
  other arithmetic  197 us (28%)
  matrix products  79.4 us (11%)
  local copies, waits for them, and re-layouts  50.7 us (7%)
  blocking collectives  48.9 us (7%)
  between operations  13.4 us (2%)
    reduce_scatter x1, waiting for transfers between devices, local(): return lax.psum_scatter(gene_flat, 'cells', scatter_dimension=0, tiled=True)  222 us
    scatter-add x8, other arithmetic, gene_turn(): return running.at[genes_here].add(product)  112 us
    all_gather x1, waiting for transfers between devices, local(): gathered = lax.all_gather(basis_rows, 'cells', axis=0, tiled=True)  82.6 us
    scatter-add x8, other arithmetic, cell_turn(): return running.at[rows_here].add(product)  72.6 us
    psum x1, blocking collectives, local(): cell_basis = lax.psum(row_flat, 'genes').astype(jnp.bfloat16)  48.9 us
    dot_general x8, matrix products, cell_turn(): jnp.einsum('sab,sbk->sak', piece, chosen, preferred_element_type=jnp.floa...  42.3 us
    dot_general x8, matrix products, gene_turn(): jnp.einsum('sab,sak->sbk', piece, chosen, preferred_element_type=jnp.floa...  37.1 us
    gather x8, local copies, waits for them, and re-layouts, cell_turn(): chosen = basis_blocks[genes_here]  31.7 us
  transfers between devices with their start and end apart: 2, of which 2 were waited for; matrix products, arithmetic and copies ran while one was open for 0% of the time, Pallas kernels for 0%

commit v1 on v0

v1 whole, which is shorter than its diff:
```python
import functools

import jax
import jax.numpy as jnp
from jax import lax
from jax.experimental import pallas as pl
from jax.experimental.pallas import tpu as pltpu
from jax.sharding import PartitionSpec as P

MESH = pl.DeviceIdType.MESH
BF = jnp.bfloat16
F32 = jnp.float32

NX, NY, NZ = 4, 4, 8
BLK = 128
RANK = 256
ROWS = 2048
COLS = 4096
CHUNK = 256
SLOTS = 320
GA = 48

ORDER = {0: 0, 1: 1, -1: 2, 2: 3, -2: 4, 3: 5, -3: 6, 4: 7}
GROUPS = ((0, 1), (1, 3), (3, 5), (5, 7), (7, 8))

NH = 1
R = RANK // NH
RA = 96 // NH
RB = R - RA
RB1 = 80 if NH == 1 else 48
N_SEM = 120 * NH


class Board:
    def __init__(self, ssem, rsem, where):
        self.ssem, self.rsem, self.where = ssem, rsem, where
        self.sent = []

    def send(self, src, dst, to):
        n = len(self.sent)
        copy = pltpu.make_async_remote_copy(
            src_ref=src, dst_ref=dst, send_sem=self.ssem.at[n], recv_sem=self.rsem.at[n],
            device_id=self.where[to], device_id_type=MESH)
        copy.start()
        self.sent.append(copy)
        return copy


def kernel(slot_ref, tiles_hbm, basis, out, tiles, xd, q, p, pcr, yr, cbt, zt,
           za, zb, as_p, as_m, ar_p, ar_m, bs, br, axr, bzr_p, bzr_m, ssem, rsem, tsem):
    c = lax.axis_index("cells")
    g = lax.axis_index("genes")
    z, x = c // NX, c % NX
    y, core = g // 2, g % 2

    def at(dz, dx, dy, dc):
        return (((z + dz + NZ) % NZ) * NX + (x + dx + NX) % NX,
                ((y + dy + NY) % NY) * 2 + (core + dc) % 2)

    where = {
        "x+": at(0, 1, 0, 0), "x-": at(0, -1, 0, 0),
        "z+": at(1, 0, 0, 0), "z-": at(-1, 0, 0, 0),
        "y+": at(0, 0, 1, 0), "y-": at(0, 0, -1, 0),
        "c": at(0, 0, 0, 1),
    }
    board = Board(ssem, rsem, where)
    send = board.send

    n_loads = 8
    per = SLOTS // n_loads
    loads = [pltpu.make_async_copy(tiles_hbm.at[pl.ds(i * per, per)],
                                   tiles.at[pl.ds(i * per, per)], tsem.at[i]) for i in range(n_loads)]
    for load in loads:
        load.start()

    barrier = pltpu.get_barrier_semaphore()
    for to in where.values():
        pl.semaphore_signal(barrier, inc=1, device_id=to, device_id_type=MESH)
    q[0, 0] = basis[...]
    tiles[SLOTS] = jnp.zeros((BLK, BLK), BF)
    pl.semaphore_wait(barrier, len(where))

    def densify(lo, hi):
        def row(r, carry):
            for col in range(lo * 4, hi * 4):
                s = slot_ref[r * 32 + col]
                xd[pl.ds(pl.multiple_of(r * BLK, BLK), BLK), col * BLK:(col + 1) * BLK] = tiles[s]
            return carry
        lax.fori_loop(0, ROWS // BLK, row, 0)

    def gather(h):
        hs = slice(h * R, (h + 1) * R)
        a, b = slice(0, GA), slice(GA, BLK)
        cut = {0: GA + 48, 1: GA + 32}
        m = {}

        def bx(k):
            lo, hi = GROUPS[k]
            m["bx+", k] = send(q.at[lo:hi, 0, b, hs], q.at[lo:hi, 3, b, hs], "x+")
            m["bx-", k] = send(q.at[lo:hi, 0, b, hs], q.at[lo:hi, 1, b, hs], "x-")

        def bxf(k):
            lo, hi = GROUPS[k]
            e = cut[k % 2]
            m["bx+", k].wait_recv()
            m["bf+", k] = send(q.at[lo:hi, 3, GA:e, hs], q.at[lo:hi, 2, GA:e, hs], "x+")
            m["bx-", k].wait_recv()
            m["bf-", k] = send(q.at[lo:hi, 1, e:BLK, hs], q.at[lo:hi, 2, e:BLK, hs], "x-")

        def az(d):
            lo, hi = (0, 4) if d < 4 else (0, 2)
            m["az+", d] = send(q.at[ORDER[1 - d], lo:hi, a, hs],
                               q.at[ORDER[-d if d < 4 else 4], lo:hi, a, hs], "z+")
            lo, hi = (0, 4) if d < 4 else (2, 4)
            m["az-", d] = send(q.at[ORDER[d - 1], lo:hi, a, hs], q.at[ORDER[d], lo:hi, a, hs], "z-")

        def bz(d):
            e = BLK if d < 4 else GA + 48
            m["bz+", d] = send(q.at[ORDER[1 - d], 0, GA:e, hs],
                               q.at[ORDER[-d if d < 4 else 4], 0, GA:e, hs], "z+")
            s = GA if d < 4 else GA + 48
            m["bz-", d] = send(q.at[ORDER[d - 1], 0, s:BLK, hs], q.at[ORDER[d], 0, s:BLK, hs], "z-")

        def wait(kind, d):
            m[kind + "+", d].wait_recv()
            m[kind + "-", d].wait_recv()

        m["ax+"] = send(q.at[0, 0, a, hs], q.at[0, 3, a, hs], "x+")
        m["ax-"] = send(q.at[0, 0, a, hs], q.at[0, 1, a, hs], "x-")
        bz(1)
        bx(0)
        if h == 0:
            for load in loads:
                load.wait()
            densify(*GROUPS[0])
        yield
        m["ax+"].wait_recv()
        m["af+"] = send(q.at[0, 3, 0:32, hs], q.at[0, 2, 0:32, hs], "x+")
        m["ax-"].wait_recv()
        m["af-"] = send(q.at[0, 1, 32:GA, hs], q.at[0, 2, 32:GA, hs], "x-")
        wait("bz", 1)
        bz(2)
        bx(1)
        m["af+"].wait_recv()
        m["af-"].wait_recv()
        az(1)
        bxf(0)
        if h == 0:
            densify(*GROUPS[1])
        yield
        wait("az", 1)
        az(2)
        wait("bz", 2)
        bz(3)
        bx(2)
        bxf(1)
        wait("bf", 0)
        if h == 0:
            densify(*GROUPS[2])
        cells_group(0, h)
        yield
        wait("az", 2)
        az(3)
        wait("bz", 3)
        bz(4)
        bx(3)
        bxf(2)
        wait("bf", 1)
        if h == 0:
            densify(*GROUPS[3])
        cells_group(1, h)
        yield
        wait("az", 3)
        az(4)
        wait("bz", 4)
        bx(4)
        bxf(3)
        wait("bf", 2)
        if h == 0:
            densify(*GROUPS[4])
        cells_group(2, h)
        yield
        bxf(4)
        wait("bf", 3)
        cells_group(3, h)
        wait("az", 4)
        wait("bf", 4)
        yield

    def cells_dot(rows, k, h):
        lo, hi = GROUPS[k]
        right = q[lo:hi, :, :, h * R:(h + 1) * R].reshape((hi - lo) * 512, R)
        return jnp.dot(xd[rows, lo * 512:hi * 512], right, preferred_element_type=F32)

    def cells_group(k, h):
        hs = slice(h * R, (h + 1) * R)

        def step(i, carry):
            rows = pl.ds(pl.multiple_of(i * 512, 512), 512)
            part = cells_dot(rows, k, h)
            p[rows, hs] = part if k == 0 else p[rows, hs] + part
            return carry
        lax.fori_loop(0, ROWS // 512, step, 0)

    def reduce_cells(h):
        hs = slice(h * R, (h + 1) * R)
        half = CHUNK // 2
        pair, m = [], {}

        def last(i):
            rows = slice(i * CHUNK, (i + 1) * CHUNK)
            return p[rows, hs] + cells_dot(rows, 4, h)

        for i in range(4):
            rows = slice(i * CHUNK, (i + 1) * CHUNK)
            p[rows, hs] = last(i)
            pair.append(send(p.at[rows, hs], pcr.at[i, :, hs], "c"))
        yield
        lows = [slice((4 + i) * CHUNK, (4 + i) * CHUNK + half) for i in range(4)]
        highs = [slice((4 + i) * CHUNK + half, (5 + i) * CHUNK) for i in range(4)]

        def own(i):
            part = last(4 + i)
            pair[i].wait_recv()
            p[(4 + i) * CHUNK:(5 + i) * CHUNK, hs] = part + pcr[i, :, hs]

        own(0)
        m["h+"] = send(p.at[lows[0], hs], yr.at[0, :, hs], "y+")
        m["h-"] = send(p.at[highs[0], hs], yr.at[1, :, hs], "y-")
        own(1)
        m["s+"] = send(p.at[highs[1], hs], yr.at[2, :, hs], "y+")
        own(2)
        m["s-"] = send(p.at[lows[2], hs], yr.at[3, :, hs], "y-")
        yield
        m["h+"].wait_recv()
        p[lows[1], hs] = p[lows[1], hs] + yr[0, :, hs]
        m["f+"] = send(p.at[lows[1], hs], yr.at[4, :, hs], "y+")
        m["h-"].wait_recv()
        p[highs[2], hs] = p[highs[2], hs] + yr[1, :, hs]
        m["f-"] = send(p.at[highs[2], hs], yr.at[5, :, hs], "y-")
        own(3)
        yield
        m["s+"].wait_recv()
        m["s-"].wait_recv()
        low = p[lows[3], hs] + yr[3, :, hs]
        high = p[highs[3], hs] + yr[2, :, hs]
        m["f+"].wait_recv()
        m["f-"].wait_recv()
        total = jnp.concatenate([low + yr[4, :, hs], high + yr[5, :, hs]], axis=0)

        def lanes(i):
            return slice(i * CHUNK, (i + 1) * CHUNK)

        mid = h * R + R // 2
        up, down = slice(h * R, mid), slice(mid, (h + 1) * R)
        cbt[hs, lanes(7)] = total.T.astype(BF)
        m["g+"] = send(cbt.at[hs, lanes(7)], cbt.at[hs, lanes(6)], "y+")
        m["g-"] = send(cbt.at[hs, lanes(7)], cbt.at[hs, lanes(5)], "y-")
        m["c3"] = send(cbt.at[hs, lanes(7)], cbt.at[hs, lanes(3)], "c")
        yield
        m["g+"].wait_recv()
        m["k+"] = send(cbt.at[up, lanes(6)], cbt.at[up, lanes(4)], "y+")
        m["c2"] = send(cbt.at[hs, lanes(6)], cbt.at[hs, lanes(2)], "c")
        m["g-"].wait_recv()
        m["k-"] = send(cbt.at[down, lanes(5)], cbt.at[down, lanes(4)], "y-")
        m["c1"] = send(cbt.at[hs, lanes(5)], cbt.at[hs, lanes(1)], "c")
        yield
        m["k+"].wait_recv()
        m["k-"].wait_recv()
        m["c0"] = send(cbt.at[hs, lanes(4)], cbt.at[hs, lanes(0)], "c")
        for i in range(4):
            m["c%d" % i].wait_recv()
        yield

    def reduce_genes(h):
        hs = slice(h * R, (h + 1) * R)
        a = slice(h * R, h * R + RA)
        b1 = slice(h * R + RA, h * R + RA + RB1)
        b2 = slice(h * R + RA + RB1, (h + 1) * R)
        v1, v2 = slice(0, RB1), slice(RB1, RB)
        m = {}

        def genes_group(k):
            lo, hi = GROUPS[k]
            for n in range(lo, hi):
                zt[n, hs] = jnp.dot(cbt[hs, :], xd[:, n * 512:(n + 1) * 512],
                                    preferred_element_type=F32)

        def lanes(dx):
            return slice(dx * BLK, (dx + 1) * BLK)

        def a_z(d):
            if d == 4:
                as_p[h, 3, :, 0:256] = zt[7, a, 0:256].astype(BF)
                m["az+", 4] = send(as_p.at[h, 3, :, 0:256], ar_p.at[h, 3, :, 0:256], "z+")
                as_m[h, 3, :, 0:256] = zt[7, a, 256:512].astype(BF)
                m["az-", 4] = send(as_m.at[h, 3, :, 0:256], ar_m.at[h, 3, :, 0:256], "z-")
                return
            i = d - 1
            m["az+", d + 1].wait_recv()
            if d == 3:
                as_p[h, i, :, 0:256] = (zt[ORDER[d], a, 0:256] + ar_p[h, 3, :, 0:256].astype(F32)).astype(BF)
                as_p[h, i, :, 256:512] = zt[ORDER[d], a, 256:512].astype(BF)
            else:
                as_p[h, i] = (zt[ORDER[d], a] + ar_p[h, i + 1].astype(F32)).astype(BF)
            m["az+", d] = send(as_p.at[h, i], ar_p.at[h, i], "z+")
            m["az-", d + 1].wait_recv()
            if d == 3:
                as_m[h, i, :, 0:256] = zt[ORDER[-d], a, 0:256].astype(BF)
                as_m[h, i, :, 256:512] = (zt[ORDER[-d], a, 256:512] + ar_m[h, 3, :, 0:256].astype(F32)).astype(BF)
            else:
                as_m[h, i] = (zt[ORDER[-d], a] + ar_m[h, i + 1].astype(F32)).astype(BF)
            m["az-", d] = send(as_m.at[h, i], ar_m.at[h, i], "z-")

        def b_send(kind, k, value, to):
            lo, hi = GROUPS[k]
            rows = v1 if kind in (0, 3, 4) else slice(0, RB - RB1)
            bs[h, kind, lo:hi, rows] = value.astype(BF)
            m["b", kind, k] = send(bs.at[h, kind, lo:hi, rows], br.at[h, kind, lo:hi, rows], to)

        def b_got(kind, k):
            lo, hi = GROUPS[k]
            rows = v1 if kind in (0, 3, 4) else slice(0, RB - RB1)
            m["b", kind, k].wait_recv()
            return br[h, kind, lo:hi, rows].astype(F32)

        def b_first(k):
            lo, hi = GROUPS[k]
            b_send(0, k, zt[lo:hi, b1, lanes(2)], "x+")
            b_send(1, k, zt[lo:hi, b2, lanes(2)], "x-")
            b_send(2, k, zt[lo:hi, b2, lanes(1)], "x+")
            b_send(3, k, zt[lo:hi, b1, lanes(3)], "x-")

        def b_merge(k):
            lo, hi = GROUPS[k]
            b_send(4, k, zt[lo:hi, b1, lanes(1)] + b_got(0, k), "x+")
            b_send(5, k, zt[lo:hi, b2, lanes(3)] + b_got(1, k), "x-")

        def b_total(k):
            lo, hi = GROUPS[k]
            zb[h, lo:hi, v1] = zt[lo:hi, b1, lanes(0)] + b_got(3, k) + b_got(4, k)
            zb[h, lo:hi, v2] = zt[lo:hi, b2, lanes(0)] + b_got(2, k) + b_got(5, k)

        def b_z(d):
            if d == 4:
                m["bz+", 4] = send(zb.at[h, 7, v1], bzr_p.at[h, 3, v1], "z+")
                m["bz-", 4] = send(zb.at[h, 7, v2], bzr_m.at[h, 3, v2], "z-")
                return
            i = d - 1
            up = v1 if d == 3 else slice(0, RB)
            down = v2 if d == 3 else slice(0, RB)
            m["bz+", d + 1].wait_recv()
            zb[h, ORDER[d], up] = zb[h, ORDER[d], up] + bzr_p[h, i + 1, up]
            m["bz+", d] = send(zb.at[h, ORDER[d]], bzr_p.at[h, i], "z+")
            m["bz-", d + 1].wait_recv()
            zb[h, ORDER[-d], down] = zb[h, ORDER[-d], down] + bzr_m[h, i + 1, down]
            m["bz-", d] = send(zb.at[h, ORDER[-d]], bzr_m.at[h, i], "z-")

        genes_group(4)
        a_z(4)
        b_first(4)
        yield
        genes_group(3)
        a_z(3)
        b_first(3)
        b_merge(4)
        yield
        genes_group(2)
        a_z(2)
        b_first(2)
        b_merge(3)
        b_total(4)
        b_z(4)
        yield
        genes_group(1)
        a_z(1)
        b_first(1)
        b_merge(2)
        b_total(3)
        b_z(3)
        yield
        genes_group(0)
        b_first(0)
        b_merge(1)
        b_total(2)
        b_z(2)
        m["az+", 1].wait_recv()
        m["az-", 1].wait_recv()
        za[h] = zt[0, a] + ar_p[h, 0].astype(F32) + ar_m[h, 0].astype(F32)
        r1, r2 = slice(0, RA // 2), slice(RA // 2, RA)
        m["a0"] = send(za.at[h, r1, lanes(2)], axr.at[h, 0], "x+")
        m["a1"] = send(za.at[h, r2, lanes(2)], axr.at[h, 1], "x-")
        m["a2"] = send(za.at[h, r2, lanes(1)], axr.at[h, 2], "x+")
        m["a3"] = send(za.at[h, r1, lanes(3)], axr.at[h, 3], "x-")
        yield
        b_merge(0)
        b_total(1)
        b_z(1)
        m["a0"].wait_recv()
        za[h, r1, lanes(1)] = za[h, r1, lanes(1)] + axr[h, 0]
        m["a4"] = send(za.at[h, r1, lanes(1)], axr.at[h, 4], "x+")
        m["a1"].wait_recv()
        za[h, r2, lanes(3)] = za[h, r2, lanes(3)] + axr[h, 1]
        m["a5"] = send(za.at[h, r2, lanes(3)], axr.at[h, 5], "x-")
        b_total(0)
        yield
        for i in range(2, 6):
            m["a%d" % i].wait_recv()
        top = jnp.concatenate([za[h, r1, lanes(0)] + axr[h, 3] + axr[h, 4],
                               za[h, r2, lanes(0)] + axr[h, 2] + axr[h, 5]], axis=0)
        m["bz+", 1].wait_recv()
        m["bz-", 1].wait_recv()
        bottom = zb[h, 0] + bzr_p[h, 0] + bzr_m[h, 0]
        out[:, hs] = jnp.concatenate([top, bottom], axis=0).T
        yield

    for h in range(NH):
        for _ in gather(h):
            pass
        for _ in reduce_cells(h):
            pass
        for _ in reduce_genes(h):
            pass

    for copy in board.sent:
        copy.wait_send()


def local(block_tiles, block_coords, block_counts, basis_rows):
    c, g = lax.axis_index("cells"), lax.axis_index("genes")
    z, x, y, core = c // NX, c % NX, g // 2, g % 2
    b, k = block_coords[:, 0], block_coords[:, 1]
    chunk = b // 2
    dy = (chunk % 4 - y + NY) % NY
    dy = jnp.where(dy == 0, 3, jnp.where(dy == 3, 2, 2 - dy))
    pos = jnp.where(chunk // 4 == core, 4, 0) + dy
    dz = (k // NX - z + NZ) % NZ
    dz = jnp.where(dz == 0, 0, jnp.where(dz <= 3, 2 * dz - 1, jnp.where(dz == 4, 7, 2 * (NZ - dz))))
    place = (pos * 2 + b % 2) * 32 + dz * NX + (k % NX - x + NX) % NX
    ids = jnp.arange(SLOTS, dtype=jnp.int32)
    place = jnp.where(ids < block_counts[0, 0], place, -1)
    hit = place[:, None] == jnp.arange(512, dtype=jnp.int32)[None, :]
    slots = jnp.min(jnp.where(hit, ids[:, None], SLOTS), axis=0)

    vmem = pl.BlockSpec(memory_space=pltpu.VMEM)
    return pl.pallas_call(
        kernel,
        out_shape=jax.ShapeDtypeStruct((BLK, RANK), F32),
        in_specs=[pl.BlockSpec(memory_space=pltpu.SMEM), pl.BlockSpec(memory_space=pl.ANY), vmem],
        out_specs=vmem,
        scratch_shapes=[
            pltpu.VMEM((SLOTS + 1, BLK, BLK), BF),
            pltpu.VMEM((ROWS, COLS), BF),
            pltpu.VMEM((NZ, NX, BLK, RANK), BF),
            pltpu.VMEM((ROWS, RANK), F32),
            pltpu.VMEM((4, CHUNK, RANK), F32),
            pltpu.VMEM((6, CHUNK // 2, RANK), F32),
            pltpu.VMEM((RANK, ROWS), BF),
            pltpu.VMEM((NZ, RANK, 512), F32),
            pltpu.VMEM((NH, RA, 512), F32),
            pltpu.VMEM((NH, NZ, RB, BLK), F32),
            pltpu.VMEM((NH, 4, RA, 512), BF),
            pltpu.VMEM((NH, 4, RA, 512), BF),
            pltpu.VMEM((NH, 4, RA, 512), BF),
            pltpu.VMEM((NH, 4, RA, 512), BF),
            pltpu.VMEM((NH, 6, NZ, RB1, BLK), BF),
            pltpu.VMEM((NH, 6, NZ, RB1, BLK), BF),
            pltpu.VMEM((NH, 6, RA // 2, BLK), F32),
            pltpu.VMEM((NH, 4, RB, BLK), F32),
            pltpu.VMEM((NH, 4, RB, BLK), F32),
            pltpu.SemaphoreType.DMA((N_SEM,)),
            pltpu.SemaphoreType.DMA((N_SEM,)),
            pltpu.SemaphoreType.DMA((8,)),
        ],
        compiler_params=pltpu.CompilerParams(
            collective_id=0, has_side_effects=True, vmem_limit_bytes=60 * 1024 * 1024),
        cost_estimate=pl.CostEstimate(flops=4 * ROWS * COLS * RANK, bytes_accessed=11_000_000,
                                      transcendentals=0),
    )(slots, block_tiles, basis_rows)


def solution(mesh):
    return jax.shard_map(
        local,
        mesh=mesh,
        in_specs=(
            P("cells", "genes", None),
            P("cells", "genes"),
            P("cells", "genes"),
            P(("cells", "genes"), None),
        ),
        out_specs=P(("cells", "genes"), None),
        check_vma=False,
    )
```

time: 697 us -> 92.3 us (0.13)
  waiting for transfers between devices: 306 us -> 0 us
  other arithmetic: 197 us -> 1.59 us
  Pallas kernels: 0 us -> 88.3 us
  matrix products: 79.4 us -> 0 us
  local copies, waits for them, and re-layouts: 50.7 us -> 1.57 us
  blocking collectives: 48.9 us -> 0 us
  between operations: 13.4 us -> 0.66 us
    reduce_scatter x1 -> x0, waiting for transfers between devices: 222 us -> none  [local(): return lax.psum_scatter(gene_flat, 'cells', scatter_dimension=0, tiled=True)]
    scatter-add x16 -> x0, other arithmetic: 185 us -> none  [the longest x8 112 us: gene_turn(): return running.at[genes_here].add(product)]
    pallas_call x0 -> x1, Pallas kernels: none -> 88.3 us  [local(): pl.pallas_call(kernel, out_shape=jax.ShapeDtypeStruct((BLK, RANK), F32),...]
    all_gather x1 -> x0, waiting for transfers between devices: 82.6 us -> none  [local(): gathered = lax.all_gather(basis_rows, 'cells', axis=0, tiled=True)]
    dot_general x16 -> x0, matrix products: 79.4 us -> none  [the longest x8 42.3 us: cell_turn(): jnp.einsum('sab,sbk->sak', piece, chosen, preferred_element_type=jnp.floa...]
    psum x1 -> x0, blocking collectives: 48.9 us -> none  [local(): cell_basis = lax.psum(row_flat, 'genes').astype(jnp.bfloat16)]
    gather x16 -> x0, local copies, waits for them, and re-layouts: 47.3 us -> none  [the longest x8 31.7 us: cell_turn(): chosen = basis_blocks[genes_here]]
    lt x16 -> x0, other arithmetic: 10.4 us -> none  [drop_dead(): live = first_slot + jnp.arange(group_size) < live_count]
  transfers between devices with their start and end apart: 2 -> 0, of which waited for: 2 -> 0; matrix products, arithmetic and copies ran while one was open for 0% -> 0% of each run, Pallas kernels for 0% -> 0%
where the time goes in v1:
time: 92.3 us; the launch traced here: 92.1 us
  Pallas kernels  88.3 us (96%)
  other arithmetic  1.59 us (2%)
  local copies, waits for them, and re-layouts  1.57 us (2%)
    pallas_call x1, Pallas kernels, local(): pl.pallas_call(kernel, out_shape=jax.ShapeDtypeStruct((BLK, RANK), F32),...  88.3 us

profile of v1, /device:TPU:8, one launch (start us, length us, event | category | flops | bytes accessed | tf_op | source)
XLA Modules:
  0.0 92.1 jit_solution(8149606306659587890)
XLA Ops:
  0.7 0.8 fusion.12
  1.5 0.7 select_reduce_fusion.slot_ref
  2.2 88.3 %shard_map.46 = f32[128,256]{1,0:T(8,128)} custom-call(s32[512]{0:T(512)} %select_reduce_fusion.slot_ref, bf16[320,128,128]{2,1,0:T(8,128)(2,1)} %tiles_hbm.1, bf16[128,256]{1,0:T(8,128)(2,1)} %basis.1), custom_call_target="tpu_custom_call" | custom-call | flops 8589934592 | bytes 11000000 | tf_op jit(solution)/shard_map/pallas_call | solution.py:446
  90.5 1.6 %copy.7 = f32[128,256]{1,0:T(8,128)} copy(f32[128,256]{1,0:T(8,128)} %shard_map.46) | data formatting | bytes 262144

commit v2 on v1

--- a/solution.py
+++ b/solution.py
@@ -46,8 +46,8 @@
         return copy
 
 
-def kernel(slot_ref, tiles_hbm, basis, out, tiles, xd, q, p, pcr, yr, cbt, zt,
-           za, zb, as_p, as_m, ar_p, ar_m, bs, br, axr, bzr_p, bzr_m, ssem, rsem, tsem):
+def kernel(count_ref, coords, tiles_hbm, basis, out, tiles, xd, q, p, pcr, yr, cbt, zt,
+           za, zb, as_p, as_m, ar_p, ar_m, bs, br, axr, bzr_p, bzr_m, slot_v, slot_ref, ssem, rsem, tsem, slot_sem):
     c = lax.axis_index("cells")
     g = lax.axis_index("genes")
     z, x = c // NX, c % NX
@@ -78,12 +78,28 @@
         pl.semaphore_signal(barrier, inc=1, device_id=to, device_id_type=MESH)
     q[0, 0] = basis[...]
     tiles[SLOTS] = jnp.zeros((BLK, BLK), BF)
+
+    b, k = coords[0:1, :], coords[1:2, :]
+    chunk = lax.shift_right_logical(b, 1)
+    dy = ((chunk & 3) - y) & 3
+    dy = jnp.where(dy == 0, 3, jnp.where(dy == 3, 2, 2 - dy))
+    pos = jnp.where(lax.shift_right_logical(chunk, 2) == core, 4, 0) + dy
+    dz = (lax.shift_right_logical(k, 2) - z) & 7
+    dz = jnp.where(dz == 0, 0, jnp.where(dz <= 3, 2 * dz - 1, jnp.where(dz == 4, 7, 2 * (NZ - dz))))
+    place = (pos * 2 + (b & 1)) * 32 + dz * NX + (((k & 3) - x) & 3)
+    live = lax.broadcasted_iota(jnp.int32, (1, SLOTS), 1) < count_ref[...]
+    place = jnp.broadcast_to(jnp.where(live, place, -1), (8, SLOTS)).T[:, 0:1]
+    ids = lax.broadcasted_iota(jnp.int32, (SLOTS, 1), 0)
+    hit = place == lax.broadcasted_iota(jnp.int32, (SLOTS, 512), 1)
+    slot_v[...] = jnp.min(jnp.where(hit, ids, SLOTS), axis=0, keepdims=True)
+    to_smem = pltpu.make_async_copy(slot_v, slot_ref, slot_sem)
+    to_smem.start()
     pl.semaphore_wait(barrier, len(where))
 
     def densify(lo, hi):
         def row(r, carry):
             for col in range(lo * 4, hi * 4):
-                s = slot_ref[r * 32 + col]
+                s = slot_ref[0, r * 32 + col]
                 xd[pl.ds(pl.multiple_of(r * BLK, BLK), BLK), col * BLK:(col + 1) * BLK] = tiles[s]
             return carry
         lax.fori_loop(0, ROWS // BLK, row, 0)
@@ -129,10 +145,6 @@
         m["ax-"] = send(q.at[0, 0, a, hs], q.at[0, 1, a, hs], "x-")
         bz(1)
         bx(0)
-        if h == 0:
-            for load in loads:
-                load.wait()
-            densify(*GROUPS[0])
         yield
         m["ax+"].wait_recv()
         m["af+"] = send(q.at[0, 3, 0:32, hs], q.at[0, 2, 0:32, hs], "x+")
@@ -145,8 +157,6 @@
         m["af-"].wait_recv()
         az(1)
         bxf(0)
-        if h == 0:
-            densify(*GROUPS[1])
         yield
         wait("az", 1)
         az(2)
@@ -156,7 +166,10 @@
         bxf(1)
         wait("bf", 0)
         if h == 0:
-            densify(*GROUPS[2])
+            to_smem.wait()
+            for load in loads:
+                load.wait()
+            densify(*GROUPS[0])
         cells_group(0, h)
         yield
         wait("az", 2)
@@ -167,7 +180,7 @@
         bxf(2)
         wait("bf", 1)
         if h == 0:
-            densify(*GROUPS[3])
+            densify(*GROUPS[1])
         cells_group(1, h)
         yield
         wait("az", 3)
@@ -177,11 +190,14 @@
         bxf(3)
         wait("bf", 2)
         if h == 0:
-            densify(*GROUPS[4])
+            densify(*GROUPS[2])
         cells_group(2, h)
         yield
         bxf(4)
         wait("bf", 3)
+        if h == 0:
+            densify(*GROUPS[3])
+            densify(*GROUPS[4])
         cells_group(3, h)
         wait("az", 4)
         wait("bf", 4)
@@ -196,33 +212,50 @@
         hs = slice(h * R, (h + 1) * R)
 
         def step(i, carry):
-            rows = pl.ds(pl.multiple_of(i * 512, 512), 512)
+            rows = pl.ds(pl.multiple_of(i * 256, 256), 256)
             part = cells_dot(rows, k, h)
             p[rows, hs] = part if k == 0 else p[rows, hs] + part
             return carry
-        lax.fori_loop(0, ROWS // 512, step, 0)
+        lax.fori_loop(0, ROWS // 256, step, 0)
 
     def reduce_cells(h):
         hs = slice(h * R, (h + 1) * R)
         half = CHUNK // 2
-        pair, m = [], {}
+        m = {}
+
+        def to_pair(i, n):
+            rows = pl.ds(i * CHUNK if isinstance(i, int) else pl.multiple_of(i * CHUNK, CHUNK), CHUNK)
+            return pltpu.make_async_remote_copy(
+                src_ref=p.at[rows, hs], dst_ref=pcr.at[i, :, hs], send_sem=ssem.at[n],
+                recv_sem=rsem.at[n], device_id=where["c"], device_id_type=MESH)
+
+        first = len(board.sent)
+        pair = [to_pair(i, first + i) for i in range(4)]
+        board.sent += pair
 
         def last(i):
-            rows = slice(i * CHUNK, (i + 1) * CHUNK)
-            return p[rows, hs] + cells_dot(rows, 4, h)
-
-        for i in range(4):
-            rows = slice(i * CHUNK, (i + 1) * CHUNK)
-            p[rows, hs] = last(i)
-            pair.append(send(p.at[rows, hs], pcr.at[i, :, hs], "c"))
-        yield
+            rows = pl.ds(pl.multiple_of(i * CHUNK, CHUNK), CHUNK)
+            p[rows, hs] = p[rows, hs] + cells_dot(rows, 4, h)
+
+        def other_core(i, carry):
+            last(i)
+            to_pair(i, first + i).start()
+            return carry
+
+        def own_core(i, carry):
+            last(i)
+            return carry
+
+        lax.fori_loop(0, 4, other_core, 0)
+        yield
+        lax.fori_loop(4, 8, own_core, 0)
         lows = [slice((4 + i) * CHUNK, (4 + i) * CHUNK + half) for i in range(4)]
         highs = [slice((4 + i) * CHUNK + half, (5 + i) * CHUNK) for i in range(4)]
 
         def own(i):
-            part = last(4 + i)
+            rows = slice((4 + i) * CHUNK, (5 + i) * CHUNK)
             pair[i].wait_recv()
-            p[(4 + i) * CHUNK:(5 + i) * CHUNK, hs] = part + pcr[i, :, hs]
+            p[rows, hs] = p[rows, hs] + pcr[i, :, hs]
 
         own(0)
         m["h+"] = send(p.at[lows[0], hs], yr.at[0, :, hs], "y+")
@@ -280,36 +313,42 @@
         v1, v2 = slice(0, RB1), slice(RB1, RB)
         m = {}
 
-        def genes_group(k):
-            lo, hi = GROUPS[k]
-            for n in range(lo, hi):
-                zt[n, hs] = jnp.dot(cbt[hs, :], xd[:, n * 512:(n + 1) * 512],
-                                    preferred_element_type=F32)
+        def genes(lo, hi):
+            def step(i, carry):
+                cols = pl.ds(pl.multiple_of(i * 256, 256), 256)
+                zt[i // 2, i % 2, hs] = jnp.dot(cbt[hs, :], xd[:, cols], preferred_element_type=F32)
+                return carry
+            lax.fori_loop(lo * 2, hi * 2, step, 0)
 
         def lanes(dx):
             return slice(dx * BLK, (dx + 1) * BLK)
 
+        def part(n, rows, dx):
+            return zt[n, dx // 2, rows, lanes(dx % 2)]
+
         def a_z(d):
             if d == 4:
-                as_p[h, 3, :, 0:256] = zt[7, a, 0:256].astype(BF)
+                as_p[h, 3, :, 0:256] = zt[7, 0, a].astype(BF)
                 m["az+", 4] = send(as_p.at[h, 3, :, 0:256], ar_p.at[h, 3, :, 0:256], "z+")
-                as_m[h, 3, :, 0:256] = zt[7, a, 256:512].astype(BF)
+                as_m[h, 3, :, 0:256] = zt[7, 1, a].astype(BF)
                 m["az-", 4] = send(as_m.at[h, 3, :, 0:256], ar_m.at[h, 3, :, 0:256], "z-")
                 return
             i = d - 1
             m["az+", d + 1].wait_recv()
-            if d == 3:
-                as_p[h, i, :, 0:256] = (zt[ORDER[d], a, 0:256] + ar_p[h, 3, :, 0:256].astype(F32)).astype(BF)
-                as_p[h, i, :, 256:512] = zt[ORDER[d], a, 256:512].astype(BF)
-            else:
-                as_p[h, i] = (zt[ORDER[d], a] + ar_p[h, i + 1].astype(F32)).astype(BF)
+            lo, hi = slice(0, 256), slice(256, 512)
+            as_p[h, i, :, lo] = (zt[ORDER[d], 0, a] + ar_p[h, i + 1, :, lo].astype(F32)).astype(BF)
+            high = zt[ORDER[d], 1, a]
+            if d < 3:
+                high = high + ar_p[h, i + 1, :, hi].astype(F32)
+            as_p[h, i, :, hi] = high.astype(BF)
             m["az+", d] = send(as_p.at[h, i], ar_p.at[h, i], "z+")
             m["az-", d + 1].wait_recv()
-            if d == 3:
-                as_m[h, i, :, 0:256] = zt[ORDER[-d], a, 0:256].astype(BF)
-                as_m[h, i, :, 256:512] = (zt[ORDER[-d], a, 256:512] + ar_m[h, 3, :, 0:256].astype(F32)).astype(BF)
-            else:
-                as_m[h, i] = (zt[ORDER[-d], a] + ar_m[h, i + 1].astype(F32)).astype(BF)
+            low = zt[ORDER[-d], 0, a]
+            if d < 3:
+                low = low + ar_m[h, i + 1, :, lo].astype(F32)
+            as_m[h, i, :, lo] = low.astype(BF)
+            far = lo if d == 3 else hi
+            as_m[h, i, :, hi] = (zt[ORDER[-d], 1, a] + ar_m[h, i + 1, :, far].astype(F32)).astype(BF)
             m["az-", d] = send(as_m.at[h, i], ar_m.at[h, i], "z-")
 
         def b_send(kind, k, value, to):
@@ -326,20 +365,20 @@
 
         def b_first(k):
             lo, hi = GROUPS[k]
-            b_send(0, k, zt[lo:hi, b1, lanes(2)], "x+")
-            b_send(1, k, zt[lo:hi, b2, lanes(2)], "x-")
-            b_send(2, k, zt[lo:hi, b2, lanes(1)], "x+")
-            b_send(3, k, zt[lo:hi, b1, lanes(3)], "x-")
+            b_send(0, k, part(slice(lo, hi), b1, 2), "x+")
+            b_send(1, k, part(slice(lo, hi), b2, 2), "x-")
+            b_send(2, k, part(slice(lo, hi), b2, 1), "x+")
+            b_send(3, k, part(slice(lo, hi), b1, 3), "x-")
 
         def b_merge(k):
             lo, hi = GROUPS[k]
-            b_send(4, k, zt[lo:hi, b1, lanes(1)] + b_got(0, k), "x+")
-            b_send(5, k, zt[lo:hi, b2, lanes(3)] + b_got(1, k), "x-")
+            b_send(4, k, part(slice(lo, hi), b1, 1) + b_got(0, k), "x+")
+            b_send(5, k, part(slice(lo, hi), b2, 3) + b_got(1, k), "x-")
 
         def b_total(k):
             lo, hi = GROUPS[k]
-            zb[h, lo:hi, v1] = zt[lo:hi, b1, lanes(0)] + b_got(3, k) + b_got(4, k)
-            zb[h, lo:hi, v2] = zt[lo:hi, b2, lanes(0)] + b_got(2, k) + b_got(5, k)
+            zb[h, lo:hi, v1] = part(slice(lo, hi), b1, 0) + b_got(3, k) + b_got(4, k)
+            zb[h, lo:hi, v2] = part(slice(lo, hi), b2, 0) + b_got(2, k) + b_got(5, k)
 
         def b_z(d):
             if d == 4:
@@ -356,37 +395,38 @@
             zb[h, ORDER[-d], down] = zb[h, ORDER[-d], down] + bzr_m[h, i + 1, down]
             m["bz-", d] = send(zb.at[h, ORDER[-d]], bzr_m.at[h, i], "z-")
 
-        genes_group(4)
+        genes(7, 8)
         a_z(4)
         b_first(4)
         yield
-        genes_group(3)
+        genes(5, 7)
         a_z(3)
         b_first(3)
         b_merge(4)
         yield
-        genes_group(2)
+        genes(3, 5)
         a_z(2)
         b_first(2)
         b_merge(3)
         b_total(4)
         b_z(4)
         yield
-        genes_group(1)
+        genes(0, 3)
         a_z(1)
         b_first(1)
         b_merge(2)
         b_total(3)
         b_z(3)
         yield
-        genes_group(0)
         b_first(0)
         b_merge(1)
         b_total(2)
         b_z(2)
         m["az+", 1].wait_recv()
         m["az-", 1].wait_recv()
-        za[h] = zt[0, a] + ar_p[h, 0].astype(F32) + ar_m[h, 0].astype(F32)
+        for i in range(2):
+            cols = slice(i * 256, (i + 1) * 256)
+            za[h, :, cols] = zt[0, i, a] + ar_p[h, 0, :, cols].astype(F32) + ar_m[h, 0, :, cols].astype(F32)
         r1, r2 = slice(0, RA // 2), slice(RA // 2, RA)
         m["a0"] = send(za.at[h, r1, lanes(2)], axr.at[h, 0], "x+")
         m["a1"] = send(za.at[h, r2, lanes(2)], axr.at[h, 1], "x-")
@@ -415,38 +455,20 @@
         yield
 
     for h in range(NH):
-        for _ in gather(h):
-            pass
-        for _ in reduce_cells(h):
-            pass
-        for _ in reduce_genes(h):
-            pass
+        for stage in (gather, reduce_cells, reduce_genes):
+            for _ in stage(h):
+                pass
 
     for copy in board.sent:
         copy.wait_send()
 
 
 def local(block_tiles, block_coords, block_counts, basis_rows):
-    c, g = lax.axis_index("cells"), lax.axis_index("genes")
-    z, x, y, core = c // NX, c % NX, g // 2, g % 2
-    b, k = block_coords[:, 0], block_coords[:, 1]
-    chunk = b // 2
-    dy = (chunk % 4 - y + NY) % NY
-    dy = jnp.where(dy == 0, 3, jnp.where(dy == 3, 2, 2 - dy))
-    pos = jnp.where(chunk // 4 == core, 4, 0) + dy
-    dz = (k // NX - z + NZ) % NZ
-    dz = jnp.where(dz == 0, 0, jnp.where(dz <= 3, 2 * dz - 1, jnp.where(dz == 4, 7, 2 * (NZ - dz))))
-    place = (pos * 2 + b % 2) * 32 + dz * NX + (k % NX - x + NX) % NX
-    ids = jnp.arange(SLOTS, dtype=jnp.int32)
-    place = jnp.where(ids < block_counts[0, 0], place, -1)
-    hit = place[:, None] == jnp.arange(512, dtype=jnp.int32)[None, :]
-    slots = jnp.min(jnp.where(hit, ids[:, None], SLOTS), axis=0)
-
     vmem = pl.BlockSpec(memory_space=pltpu.VMEM)
     return pl.pallas_call(
         kernel,
         out_shape=jax.ShapeDtypeStruct((BLK, RANK), F32),
-        in_specs=[pl.BlockSpec(memory_space=pltpu.SMEM), pl.BlockSpec(memory_space=pl.ANY), vmem],
+        in_specs=[vmem, vmem, pl.BlockSpec(memory_space=pl.ANY), vmem],
         out_specs=vmem,
         scratch_shapes=[
             pltpu.VMEM((SLOTS + 1, BLK, BLK), BF),
@@ -456,7 +478,7 @@
             pltpu.VMEM((4, CHUNK, RANK), F32),
             pltpu.VMEM((6, CHUNK // 2, RANK), F32),
             pltpu.VMEM((RANK, ROWS), BF),
-            pltpu.VMEM((NZ, RANK, 512), F32),
+            pltpu.VMEM((NZ, 2, RANK, 256), F32),
             pltpu.VMEM((NH, RA, 512), F32),
             pltpu.VMEM((NH, NZ, RB, BLK), F32),
             pltpu.VMEM((NH, 4, RA, 512), BF),
@@ -468,15 +490,18 @@
             pltpu.VMEM((NH, 6, RA // 2, BLK), F32),
             pltpu.VMEM((NH, 4, RB, BLK), F32),
             pltpu.VMEM((NH, 4, RB, BLK), F32),
+            pltpu.VMEM((1, 512), jnp.int32),
+            pltpu.SMEM((1, 512), jnp.int32),
             pltpu.SemaphoreType.DMA((N_SEM,)),
             pltpu.SemaphoreType.DMA((N_SEM,)),
             pltpu.SemaphoreType.DMA((8,)),
+            pltpu.SemaphoreType.DMA,
         ],
         compiler_params=pltpu.CompilerParams(
             collective_id=0, has_side_effects=True, vmem_limit_bytes=60 * 1024 * 1024),
         cost_estimate=pl.CostEstimate(flops=4 * ROWS * COLS * RANK, bytes_accessed=11_000_000,
                                       transcendentals=0),
-    )(slots, block_tiles, basis_rows)
+    )(block_counts, block_coords.T, block_tiles, basis_rows)
 
 
 def solution(mesh):

time: 92.3 us -> 91.8 us (level)
  other arithmetic: 1.59 us -> 0 us
  Pallas kernels: 88.3 us -> 89.5 us
    pallas_call x1, Pallas kernels: 88.3 us -> 89.5 us  [local(): pl.pallas_call(kernel, out_shape=jax.ShapeDtypeStruct((BLK, RANK), F32),...]
where the time goes in v2:
time: 91.8 us; the launch traced here: 91.7 us
  Pallas kernels  89.5 us (97%)
  local copies, waits for them, and re-layouts  1.57 us (2%)
    pallas_call x1, Pallas kernels, local(): pl.pallas_call(kernel, out_shape=jax.ShapeDtypeStruct((BLK, RANK), F32),...  89.5 us

profile of v2, /device:TPU:8, one launch (start us, length us, event | category | flops | bytes accessed | tf_op | source)
XLA Modules:
  0.0 91.7 jit_solution(11271524240554669891)
XLA Ops:
  0.7 89.5 %shard_map.46 = f32[128,256]{1,0:T(8,128)} custom-call(s32[1,1]{1,0:T(1,128)S(6)} %copy.6.count_ref, s32[2,320]{1,0:T(2,128)} %bitcast.1, bf16[320,128,128]{2,1,0:T(8,128)(2,1)} %tiles_hbm.1, bf16[128,256]{1,0:T(8,128)(2,1)} %basis.1), custom_call_target="tpu_custom_call" | custom-call | flops 8589934592 | bytes 11000000 | tf_op jit(solution)/shard_map/pallas_call | solution.py:468
  90.1 1.6 %copy.7 = f32[128,256]{1,0:T(8,128)} copy(f32[128,256]{1,0:T(8,128)} %shard_map.46) | data formatting | bytes 262144

commit v3 on v2

--- a/solution.py
+++ b/solution.py
@@ -46,8 +46,8 @@
         return copy
 
 
-def kernel(count_ref, coords, tiles_hbm, basis, out, tiles, xd, q, p, pcr, yr, cbt, zt,
-           za, zb, as_p, as_m, ar_p, ar_m, bs, br, axr, bzr_p, bzr_m, slot_v, slot_ref, ssem, rsem, tsem, slot_sem):
+def gather_kernel(count_ref, coords, tiles_hbm, basis, q, xd_out, tiles, xd,
+                  slot_v, slot_ref, ssem, rsem, tsem, slot_sem, out_sem):
     c = lax.axis_index("cells")
     g = lax.axis_index("genes")
     z, x = c // NX, c % NX
@@ -169,8 +169,7 @@
             to_smem.wait()
             for load in loads:
                 load.wait()
-            densify(*GROUPS[0])
-        cells_group(0, h)
+            densify(0, 2)
         yield
         wait("az", 2)
         az(3)
@@ -180,8 +179,7 @@
         bxf(2)
         wait("bf", 1)
         if h == 0:
-            densify(*GROUPS[1])
-        cells_group(1, h)
+            densify(2, 4)
         yield
         wait("az", 3)
         az(4)
@@ -190,33 +188,48 @@
         bxf(3)
         wait("bf", 2)
         if h == 0:
-            densify(*GROUPS[2])
-        cells_group(2, h)
+            densify(4, 6)
         yield
         bxf(4)
         wait("bf", 3)
         if h == 0:
-            densify(*GROUPS[3])
-            densify(*GROUPS[4])
-        cells_group(3, h)
+            densify(6, 8)
+            to_hbm = pltpu.make_async_copy(xd, xd_out, out_sem)
+            to_hbm.start()
+            to_hbm.wait()
         wait("az", 4)
         wait("bf", 4)
         yield
 
-    def cells_dot(rows, k, h):
-        lo, hi = GROUPS[k]
-        right = q[lo:hi, :, :, h * R:(h + 1) * R].reshape((hi - lo) * 512, R)
-        return jnp.dot(xd[rows, lo * 512:hi * 512], right, preferred_element_type=F32)
-
-    def cells_group(k, h):
-        hs = slice(h * R, (h + 1) * R)
-
-        def step(i, carry):
-            rows = pl.ds(pl.multiple_of(i * 256, 256), 256)
-            part = cells_dot(rows, k, h)
-            p[rows, hs] = part if k == 0 else p[rows, hs] + part
-            return carry
-        lax.fori_loop(0, ROWS // 256, step, 0)
+    for _ in gather(0):
+        pass
+    for copy in board.sent:
+        copy.wait_send()
+
+
+def cells_kernel(p_in, cbt, p, pcr, yr, ssem, rsem):
+    c = lax.axis_index("cells")
+    g = lax.axis_index("genes")
+    z, x = c // NX, c % NX
+    y, core = g // 2, g % 2
+
+    def at(dz, dx, dy, dc):
+        return (((z + dz + NZ) % NZ) * NX + (x + dx + NX) % NX,
+                ((y + dy + NY) % NY) * 2 + (core + dc) % 2)
+
+    where = {
+        "x+": at(0, 1, 0, 0), "x-": at(0, -1, 0, 0),
+        "z+": at(1, 0, 0, 0), "z-": at(-1, 0, 0, 0),
+        "y+": at(0, 0, 1, 0), "y-": at(0, 0, -1, 0),
+        "c": at(0, 0, 0, 1),
+    }
+    board = Board(ssem, rsem, where)
+    send = board.send
+
+    barrier = pltpu.get_barrier_semaphore()
+    for to in where.values():
+        pl.semaphore_signal(barrier, inc=1, device_id=to, device_id_type=MESH)
+    pl.semaphore_wait(barrier, len(where))
 
     def reduce_cells(h):
         hs = slice(h * R, (h + 1) * R)
@@ -226,36 +239,24 @@
         def to_pair(i, n):
             rows = pl.ds(i * CHUNK if isinstance(i, int) else pl.multiple_of(i * CHUNK, CHUNK), CHUNK)
             return pltpu.make_async_remote_copy(
-                src_ref=p.at[rows, hs], dst_ref=pcr.at[i, :, hs], send_sem=ssem.at[n],
+                src_ref=p_in.at[rows, hs], dst_ref=pcr.at[i, :, hs], send_sem=ssem.at[n],
                 recv_sem=rsem.at[n], device_id=where["c"], device_id_type=MESH)
 
         first = len(board.sent)
         pair = [to_pair(i, first + i) for i in range(4)]
         board.sent += pair
 
-        def last(i):
-            rows = pl.ds(pl.multiple_of(i * CHUNK, CHUNK), CHUNK)
-            p[rows, hs] = p[rows, hs] + cells_dot(rows, 4, h)
-
-        def other_core(i, carry):
-            last(i)
-            to_pair(i, first + i).start()
-            return carry
-
-        def own_core(i, carry):
-            last(i)
-            return carry
-
-        lax.fori_loop(0, 4, other_core, 0)
-        yield
-        lax.fori_loop(4, 8, own_core, 0)
+        for copy in pair:
+            copy.start()
+        yield
+
         lows = [slice((4 + i) * CHUNK, (4 + i) * CHUNK + half) for i in range(4)]
         highs = [slice((4 + i) * CHUNK + half, (5 + i) * CHUNK) for i in range(4)]
 
         def own(i):
             rows = slice((4 + i) * CHUNK, (5 + i) * CHUNK)
             pair[i].wait_recv()
-            p[rows, hs] = p[rows, hs] + pcr[i, :, hs]
+            p[rows, hs] = p_in[rows, hs] + pcr[i, :, hs]
 
         own(0)
         m["h+"] = send(p.at[lows[0], hs], yr.at[0, :, hs], "y+")
@@ -305,6 +306,36 @@
             m["c%d" % i].wait_recv()
         yield
 
+    for _ in reduce_cells(0):
+        pass
+    for copy in board.sent:
+        copy.wait_send()
+
+
+def genes_kernel(zt, out, za, zb, as_p, as_m, ar_p, ar_m, bs, br, axr, bzr_p, bzr_m, ssem, rsem):
+    c = lax.axis_index("cells")
+    g = lax.axis_index("genes")
+    z, x = c // NX, c % NX
+    y, core = g // 2, g % 2
+
+    def at(dz, dx, dy, dc):
+        return (((z + dz + NZ) % NZ) * NX + (x + dx + NX) % NX,
+                ((y + dy + NY) % NY) * 2 + (core + dc) % 2)
+
+    where = {
+        "x+": at(0, 1, 0, 0), "x-": at(0, -1, 0, 0),
+        "z+": at(1, 0, 0, 0), "z-": at(-1, 0, 0, 0),
+        "y+": at(0, 0, 1, 0), "y-": at(0, 0, -1, 0),
+        "c": at(0, 0, 0, 1),
+    }
+    board = Board(ssem, rsem, where)
+    send = board.send
+
+    barrier = pltpu.get_barrier_semaphore()
+    for to in where.values():
+        pl.semaphore_signal(barrier, inc=1, device_id=to, device_id_type=MESH)
+    pl.semaphore_wait(barrier, len(where))
+
     def reduce_genes(h):
         hs = slice(h * R, (h + 1) * R)
         a = slice(h * R, h * R + RA)
@@ -313,42 +344,39 @@
         v1, v2 = slice(0, RB1), slice(RB1, RB)
         m = {}
 
-        def genes(lo, hi):
-            def step(i, carry):
-                cols = pl.ds(pl.multiple_of(i * 256, 256), 256)
-                zt[i // 2, i % 2, hs] = jnp.dot(cbt[hs, :], xd[:, cols], preferred_element_type=F32)
-                return carry
-            lax.fori_loop(lo * 2, hi * 2, step, 0)
-
         def lanes(dx):
             return slice(dx * BLK, (dx + 1) * BLK)
 
+        def plane(n, i):
+            return zt[a, n * 512 + i * 256:n * 512 + (i + 1) * 256]
+
         def part(n, rows, dx):
-            return zt[n, dx // 2, rows, lanes(dx % 2)]
+            return jnp.stack([zt[rows, i * 512 + dx * BLK:i * 512 + (dx + 1) * BLK]
+                              for i in range(n.start, n.stop)])
 
         def a_z(d):
             if d == 4:
-                as_p[h, 3, :, 0:256] = zt[7, 0, a].astype(BF)
+                as_p[h, 3, :, 0:256] = plane(7, 0).astype(BF)
                 m["az+", 4] = send(as_p.at[h, 3, :, 0:256], ar_p.at[h, 3, :, 0:256], "z+")
-                as_m[h, 3, :, 0:256] = zt[7, 1, a].astype(BF)
+                as_m[h, 3, :, 0:256] = plane(7, 1).astype(BF)
                 m["az-", 4] = send(as_m.at[h, 3, :, 0:256], ar_m.at[h, 3, :, 0:256], "z-")
                 return
             i = d - 1
             m["az+", d + 1].wait_recv()
             lo, hi = slice(0, 256), slice(256, 512)
-            as_p[h, i, :, lo] = (zt[ORDER[d], 0, a] + ar_p[h, i + 1, :, lo].astype(F32)).astype(BF)
-            high = zt[ORDER[d], 1, a]
+            as_p[h, i, :, lo] = (plane(ORDER[d], 0) + ar_p[h, i + 1, :, lo].astype(F32)).astype(BF)
+            high = plane(ORDER[d], 1)
             if d < 3:
                 high = high + ar_p[h, i + 1, :, hi].astype(F32)
             as_p[h, i, :, hi] = high.astype(BF)
             m["az+", d] = send(as_p.at[h, i], ar_p.at[h, i], "z+")
             m["az-", d + 1].wait_recv()
-            low = zt[ORDER[-d], 0, a]
+            low = plane(ORDER[-d], 0)
             if d < 3:
                 low = low + ar_m[h, i + 1, :, lo].astype(F32)
             as_m[h, i, :, lo] = low.astype(BF)
             far = lo if d == 3 else hi
-            as_m[h, i, :, hi] = (zt[ORDER[-d], 1, a] + ar_m[h, i + 1, :, far].astype(F32)).astype(BF)
+            as_m[h, i, :, hi] = (plane(ORDER[-d], 1) + ar_m[h, i + 1, :, far].astype(F32)).astype(BF)
             m["az-", d] = send(as_m.at[h, i], ar_m.at[h, i], "z-")
 
         def b_send(kind, k, value, to):
@@ -395,23 +423,19 @@
             zb[h, ORDER[-d], down] = zb[h, ORDER[-d], down] + bzr_m[h, i + 1, down]
             m["bz-", d] = send(zb.at[h, ORDER[-d]], bzr_m.at[h, i], "z-")
 
-        genes(7, 8)
         a_z(4)
         b_first(4)
         yield
-        genes(5, 7)
         a_z(3)
         b_first(3)
         b_merge(4)
         yield
-        genes(3, 5)
         a_z(2)
         b_first(2)
         b_merge(3)
         b_total(4)
         b_z(4)
         yield
-        genes(0, 3)
         a_z(1)
         b_first(1)
         b_merge(2)
@@ -426,7 +450,7 @@
         m["az-", 1].wait_recv()
         for i in range(2):
             cols = slice(i * 256, (i + 1) * 256)
-            za[h, :, cols] = zt[0, i, a] + ar_p[h, 0, :, cols].astype(F32) + ar_m[h, 0, :, cols].astype(F32)
+            za[h, :, cols] = plane(0, i) + ar_p[h, 0, :, cols].astype(F32) + ar_m[h, 0, :, cols].astype(F32)
         r1, r2 = slice(0, RA // 2), slice(RA // 2, RA)
         m["a0"] = send(za.at[h, r1, lanes(2)], axr.at[h, 0], "x+")
         m["a1"] = send(za.at[h, r2, lanes(2)], axr.at[h, 1], "x-")
@@ -454,54 +478,55 @@
         out[:, hs] = jnp.concatenate([top, bottom], axis=0).T
         yield
 
-    for h in range(NH):
-        for stage in (gather, reduce_cells, reduce_genes):
-            for _ in stage(h):
-                pass
-
+    for _ in reduce_genes(0):
+        pass
     for copy in board.sent:
         copy.wait_send()
 
 
-def local(block_tiles, block_coords, block_counts, basis_rows):
+def call(kernel, n, outs, ins, scratch):
     vmem = pl.BlockSpec(memory_space=pltpu.VMEM)
     return pl.pallas_call(
         kernel,
-        out_shape=jax.ShapeDtypeStruct((BLK, RANK), F32),
-        in_specs=[vmem, vmem, pl.BlockSpec(memory_space=pl.ANY), vmem],
-        out_specs=vmem,
-        scratch_shapes=[
-            pltpu.VMEM((SLOTS + 1, BLK, BLK), BF),
-            pltpu.VMEM((ROWS, COLS), BF),
-            pltpu.VMEM((NZ, NX, BLK, RANK), BF),
-            pltpu.VMEM((ROWS, RANK), F32),
-            pltpu.VMEM((4, CHUNK, RANK), F32),
-            pltpu.VMEM((6, CHUNK // 2, RANK), F32),
-            pltpu.VMEM((RANK, ROWS), BF),
-            pltpu.VMEM((NZ, 2, RANK, 256), F32),
-            pltpu.VMEM((NH, RA, 512), F32),
-            pltpu.VMEM((NH, NZ, RB, BLK), F32),
-            pltpu.VMEM((NH, 4, RA, 512), BF),
-            pltpu.VMEM((NH, 4, RA, 512), BF),
-            pltpu.VMEM((NH, 4, RA, 512), BF),
-            pltpu.VMEM((NH, 4, RA, 512), BF),
-            pltpu.VMEM((NH, 6, NZ, RB1, BLK), BF),
-            pltpu.VMEM((NH, 6, NZ, RB1, BLK), BF),
-            pltpu.VMEM((NH, 6, RA // 2, BLK), F32),
-            pltpu.VMEM((NH, 4, RB, BLK), F32),
-            pltpu.VMEM((NH, 4, RB, BLK), F32),
-            pltpu.VMEM((1, 512), jnp.int32),
-            pltpu.SMEM((1, 512), jnp.int32),
-            pltpu.SemaphoreType.DMA((N_SEM,)),
-            pltpu.SemaphoreType.DMA((N_SEM,)),
-            pltpu.SemaphoreType.DMA((8,)),
-            pltpu.SemaphoreType.DMA,
-        ],
+        out_shape=[jax.ShapeDtypeStruct(shape, dtype) for shape, dtype, _ in outs],
+        in_specs=[pl.BlockSpec(memory_space=pl.ANY) if len(a.shape) == 3 else vmem for a in ins],
+        out_specs=[vmem if kept else pl.BlockSpec(memory_space=pl.ANY) for _, _, kept in outs],
+        scratch_shapes=scratch + [pltpu.SemaphoreType.DMA((N_SEM,)), pltpu.SemaphoreType.DMA((N_SEM,))] + (
+            [pltpu.SemaphoreType.DMA((8,)), pltpu.SemaphoreType.DMA, pltpu.SemaphoreType.DMA] if n == 0 else []),
         compiler_params=pltpu.CompilerParams(
-            collective_id=0, has_side_effects=True, vmem_limit_bytes=60 * 1024 * 1024),
-        cost_estimate=pl.CostEstimate(flops=4 * ROWS * COLS * RANK, bytes_accessed=11_000_000,
-                                      transcendentals=0),
-    )(block_counts, block_coords.T, block_tiles, basis_rows)
+            collective_id=n, has_side_effects=True, vmem_limit_bytes=60 * 1024 * 1024),
+    )(*ins)
+
+
+def local(block_tiles, block_coords, block_counts, basis_rows):
+    q, xd = call(gather_kernel, 0, [((NZ, NX, BLK, RANK), BF, True), ((ROWS, COLS), BF, False)],
+                 [block_counts, block_coords.T, block_tiles, basis_rows], [
+        pltpu.VMEM((SLOTS + 1, BLK, BLK), BF),
+        pltpu.VMEM((ROWS, COLS), BF),
+        pltpu.VMEM((1, 512), jnp.int32),
+        pltpu.SMEM((1, 512), jnp.int32),
+    ])
+    part = jnp.dot(xd, q.reshape(COLS, RANK), preferred_element_type=F32)
+    cbt, = call(cells_kernel, 1, [((RANK, ROWS), BF, True)], [part], [
+        pltpu.VMEM((ROWS, RANK), F32),
+        pltpu.VMEM((4, CHUNK, RANK), F32),
+        pltpu.VMEM((6, CHUNK // 2, RANK), F32),
+    ])
+    zt = jnp.dot(cbt, xd, preferred_element_type=F32)
+    out, = call(genes_kernel, 2, [((BLK, RANK), F32, True)], [zt], [
+        pltpu.VMEM((NH, RA, 512), F32),
+        pltpu.VMEM((NH, NZ, RB, BLK), F32),
+        pltpu.VMEM((NH, 4, RA, 512), BF),
+        pltpu.VMEM((NH, 4, RA, 512), BF),
+        pltpu.VMEM((NH, 4, RA, 512), BF),
+        pltpu.VMEM((NH, 4, RA, 512), BF),
+        pltpu.VMEM((NH, 6, NZ, RB1, BLK), BF),
+        pltpu.VMEM((NH, 6, NZ, RB1, BLK), BF),
+        pltpu.VMEM((NH, 6, RA // 2, BLK), F32),
+        pltpu.VMEM((NH, 4, RB, BLK), F32),
+        pltpu.VMEM((NH, 4, RB, BLK), F32),
+    ])
+    return out
 
 
 def solution(mesh):

time: 91.8 us -> 131 us (1.43)
  matrix products: 0 us -> 24.9 us
  Pallas kernels: 89.5 us -> 104 us
    dot_general x0 -> x2, matrix products: none -> 24.9 us  [the longest x1 12.5 us: local(): zt = jnp.dot(cbt, xd, preferred_element_type=F32)]
    pallas_call x1 -> x3, Pallas kernels: 89.5 us -> 104 us  [call(): pl.pallas_call(kernel, out_shape=[jax.ShapeDtypeStruct(shape, dtype) for...]
where the time goes in v3:
time: 131 us
  Pallas kernels  104 us (79%)
  matrix products  24.9 us (19%)
  local copies, waits for them, and re-layouts  1.57 us (1%)
    pallas_call x3, Pallas kernels, call(): pl.pallas_call(kernel, out_shape=[jax.ShapeDtypeStruct(shape, dtype) for...  104 us
    dot_general x1, matrix products, local(): zt = jnp.dot(cbt, xd, preferred_element_type=F32)  12.5 us
    dot_general x1, matrix products, local(): part = jnp.dot(xd, q.reshape(COLS, RANK), preferred_element_type=F32)  12.4 us

profile of v3, /device:TPU:8, one launch (start us, length us, event | category | flops | bytes accessed | tf_op | source)
XLA Modules:
  0.0 131.0 jit_solution(1207383914464969764)
XLA Ops:
  0.7 43.4 %shard_map.46 = (bf16[8,4,128,256]{3,2,1,0:T(8,128)(2,1)}, bf16[2048,4096]{1,0:T(8,128)(2,1)}) custom-call(s32[1,1]{1,0:T(1,128)S(6)} %copy.6.count_ref, s32[2,320]{1,0:T(2,128)} %bitcast.6, bf16[320,128,128]{2,1,0:T(8,128)(2,1)} %tiles_hbm.1, bf16[128,256]{1,0:T(8,128)(2,1)} %basis.1), custom_call_target="tpu_custom_call" | custom-call | tf_op jit(solution)/shard_map/pallas_call | solution.py:489
  44.1 12.4 %fusion.p_in = f32[2048,256]{1,0:T(8,128)} fusion(bf16[2048,4096]{1,0:T(8,128)(2,1)} %get-tuple-element.7, bf16[4096,256]{1,0:T(8,128)(2,1)} %bitcast.7), kind=kOutput, calls=%fused_computation | convolution fusion | flops 4294967296 | bytes 20971520 | tf_op jit(solution)/shard_map/dot_general | solution.py:509
  56.4 28.4 %shard_map.47 = bf16[256,2048]{1,0:T(8,128)(2,1)} custom-call(f32[2048,256]{1,0:T(8,128)} %fusion.p_in), custom_call_target="tpu_custom_call" | custom-call | tf_op jit(solution)/shard_map/pallas_call | solution.py:489
  84.9 12.5 %fusion.1.zt = f32[256,4096]{1,0:T(8,128)} fusion(bf16[256,2048]{1,0:T(8,128)(2,1)} %shard_map.47, bf16[2048,4096]{1,0:T(8,128)(2,1)} %get-tuple-element.7), kind=kOutput, calls=%fused_computation.1 | convolution fusion | flops 4294967296 | bytes 22020096 | tf_op jit(solution)/shard_map/dot_general | solution.py:515
  97.4 32.0 %shard_map.48 = f32[128,256]{1,0:T(8,128)} custom-call(f32[256,4096]{1,0:T(8,128)} %fusion.1.zt), custom_call_target="tpu_custom_call" | custom-call | tf_op jit(solution)/shard_map/pallas_call | solution.py:489
  129.5 1.6 %copy.7 = f32[128,256]{1,0:T(8,128)} copy(f32[128,256]{1,0:T(8,128)} %shard_map.48) | data formatting | bytes 262144

commit v4 on v0

v4 whole, which is shorter than its diff:
```python
import jax
import jax.numpy as jnp
import numpy as np
from jax import lax
from jax.experimental import pallas as pl
from jax.experimental.pallas import tpu as pltpu
from jax.sharding import PartitionSpec as P

MESH = pl.DeviceIdType.MESH
BF = jnp.bfloat16
F32 = jnp.float32

NX, NY, NZ = 4, 4, 8
BLK = 128
RANK = 256
ROWS = 2048
COLS = 4096
CHUNK = 256
HALF = CHUNK // 2
SLOTS = 320
GA = 48
RA = 96
RB = RANK - RA
RB1 = 80

ORDER = {0: 0, 1: 1, -1: 2, 2: 3, -2: 4, 3: 5, -3: 6, 4: 7, -4: 7}
GROUPS = ((0, 1), (1, 3), (3, 5), (5, 7), (7, 8))
SIGNS = (("+", 1), ("-", -1))

HOP = 1.5
LINK = {"x+": 50e3, "x-": 50e3, "z+": 50e3, "z-": 50e3, "y+": 50e3, "y-": 50e3, "c": 500e3}
ISSUE = 0.08
N_SEM = 136


class Plan:
    def __init__(self, ssem, rsem, where):
        self.ssem, self.rsem, self.where = ssem, rsem, where
        self.tasks = {}
        self.count = 0

    def task(self, name, needs, cost, run, message=None):
        assert name not in self.tasks, name
        self.tasks[name] = (tuple(needs), cost, run, message)

    def send(self, name, needs, src, dst, to, run=None, cost=0.0):
        copy = pltpu.make_async_remote_copy(
            src_ref=src, dst_ref=dst, send_sem=self.ssem.at[self.count],
            recv_sem=self.rsem.at[self.count], device_id=self.where[to], device_id_type=MESH)
        self.count += 1
        time = float(np.prod(src.shape)) * np.dtype(src.dtype).itemsize / LINK[to]
        self.task(name, needs, cost + ISSUE, run, (copy, to, time))

    def order(self):
        after = {name: [] for name in self.tasks}
        for name, (needs, *_) in self.tasks.items():
            for need in needs:
                after[need].append(name)
        rank = {}

        def longest(name):
            if name not in rank:
                _, cost, _, message = self.tasks[name]
                tail = max([longest(n) for n in after[name]], default=0.0)
                rank[name] = cost + (message[2] + HOP if message else 0.0) + tail
            return rank[name]

        for name in self.tasks:
            longest(name)
        now, free, ready_at, order = 0.0, {}, {}, []
        left = dict.fromkeys(self.tasks)
        while left:
            can = {n: max([ready_at[d] for d in self.tasks[n][0]], default=0.0)
                   for n in left if all(d in ready_at for d in self.tasks[n][0])}
            now = max(now, min(can.values()))
            name = max((n for n in can if can[n] <= now), key=lambda n: rank[n])
            del left[name]
            order.append(name)
            _, cost, _, message = self.tasks[name]
            now += cost
            ready_at[name] = now
            if message:
                _, to, time = message
                free[to] = max(now, free.get(to, 0.0)) + time
                ready_at[name] = free[to] + HOP
        self.finish, self.ready_at = now, ready_at
        return order

    def run(self):
        got = set()
        assert self.count <= N_SEM
        order = self.order()
        for name in order:
            needs, _, run, message = self.tasks[name]
            for need in needs:
                if self.tasks[need][3] and need not in got:
                    self.tasks[need][3][0].wait_recv()
                    got.add(need)
            if run:
                run()
            if message:
                message[0].start()
        for name in order:
            if self.tasks[name][3]:
                assert name in got, name
                self.tasks[name][3][0].wait_send()


def kernel(count_ref, coords, tiles_hbm, basis, out, tiles, xd, q, p, pcr, yr, cbt, zt,
           za, zb, azs, azr, axr, bs, br, bzr, slot_v, slot_ref, ssem, rsem, tsem, slot_sem):
    c = lax.axis_index("cells")
    g = lax.axis_index("genes")
    z, x = c // NX, c % NX
    y, core = g // 2, g % 2

    def at(dz, dx, dy, dc):
        return (((z + dz + NZ) % NZ) * NX + (x + dx + NX) % NX,
                ((y + dy + NY) % NY) * 2 + (core + dc) % 2)

    where = {
        "x+": at(0, 1, 0, 0), "x-": at(0, -1, 0, 0),
        "z+": at(1, 0, 0, 0), "z-": at(-1, 0, 0, 0),
        "y+": at(0, 0, 1, 0), "y-": at(0, 0, -1, 0),
        "c": at(0, 0, 0, 1),
    }
    plan = Plan(ssem, rsem, where)
    task, send = plan.task, plan.send

    n_loads = 8
    per = SLOTS // n_loads
    loads = [pltpu.make_async_copy(tiles_hbm.at[pl.ds(i * per, per)],
                                   tiles.at[pl.ds(i * per, per)], tsem.at[i]) for i in range(n_loads)]
    for load in loads:
        load.start()

    barrier = pltpu.get_barrier_semaphore()
    for to in where.values():
        pl.semaphore_signal(barrier, inc=1, device_id=to, device_id_type=MESH)
    q[0, 0] = basis[...]
    tiles[SLOTS] = jnp.zeros((BLK, BLK), BF)

    b, k = coords[0:1, :], coords[1:2, :]
    chunk = lax.shift_right_logical(b, 1)
    dy = ((chunk & 3) - y) & 3
    dy = jnp.where(dy == 0, 3, jnp.where(dy == 3, 2, 2 - dy))
    pos = jnp.where(lax.shift_right_logical(chunk, 2) == core, 4, 0) + dy
    dz = (lax.shift_right_logical(k, 2) - z) & 7
    dz = jnp.where(dz == 0, 0, jnp.where(dz <= 3, 2 * dz - 1, jnp.where(dz == 4, 7, 2 * (NZ - dz))))
    dx = ((k & 3) - x) & 3
    dx = jnp.where(dx >= 2, 5 - dx, dx)
    place = (pos * 2 + (b & 1)) * 32 + dz * NX + dx
    live = lax.broadcasted_iota(jnp.int32, (1, SLOTS), 1) < count_ref[...]
    place = jnp.broadcast_to(jnp.where(live, place, -1), (8, SLOTS)).T[:, 0:1]
    ids = lax.broadcasted_iota(jnp.int32, (SLOTS, 1), 0)
    hit = place == lax.broadcasted_iota(jnp.int32, (SLOTS, 512), 1)
    slot_v[...] = jnp.min(jnp.where(hit, ids, SLOTS), axis=0, keepdims=True)
    to_smem = pltpu.make_async_copy(slot_v, slot_ref, slot_sem)
    to_smem.start()
    pl.semaphore_wait(barrier, len(where))

    def densify(lo, hi):
        def row(r, carry):
            for col in range(lo * 4, hi * 4):
                s = slot_ref[0, r * 32 + col]
                xd[pl.ds(pl.multiple_of(r * BLK, BLK), BLK), col * BLK:(col + 1) * BLK] = tiles[s]
            return carry
        lax.fori_loop(0, ROWS // BLK, row, 0)

    def loaded():
        to_smem.wait()
        for load in loads:
            load.wait()

    a, b = slice(0, GA), slice(GA, BLK)
    send("ax+", [], q.at[0, 0, a], q.at[0, 2, a], "x+")
    send("ax-", [], q.at[0, 0, a], q.at[0, 1, a], "x-")
    send("af+", ["ax+"], q.at[0, 2, 0:32], q.at[0, 3, 0:32], "x+")
    send("af-", ["ax-"], q.at[0, 1, 32:GA], q.at[0, 3, 32:GA], "x-")
    for d in range(1, 5):
        for s, sign in SIGNS:
            src, dst = ORDER[-sign * (d - 1)], ORDER[-sign * d]
            last = [f"{d - 1}{s}"] if d > 1 else []
            rows = slice(0, BLK) if d < 4 else slice(0, 64) if sign > 0 else slice(64, BLK)
            send(f"zo{d}{s}", ["zo" + n for n in last], q.at[src, 0, rows], q.at[dst, 0, rows], "z" + s)
            cols = slice(1, 3) if d < 4 else slice(1, 2) if sign > 0 else slice(2, 3)
            send(f"zn{d}{s}", ["zn" + n for n in last] or ["ax+", "ax-"],
                 q.at[src, cols, a], q.at[dst, cols, a], "z" + s)
            rows = a if d < 4 else slice(0, 32) if sign > 0 else slice(32, GA)
            send(f"zf{d}{s}", ["zf" + n for n in last] or ["af+", "af-"],
                 q.at[src, 3, rows], q.at[dst, 3, rows], "z" + s)
    for k, (lo, hi) in enumerate(GROUPS):
        here = [f"zo{k}+", f"zo{k}-"] if k else []
        e = GA + (48 if k % 2 else 32)
        send(f"bx{k}+", here, q.at[lo:hi, 0, b], q.at[lo:hi, 2, b], "x+")
        send(f"bx{k}-", here, q.at[lo:hi, 0, b], q.at[lo:hi, 1, b], "x-")
        send(f"bf{k}+", [f"bx{k}+"], q.at[lo:hi, 2, GA:e], q.at[lo:hi, 3, GA:e], "x+")
        send(f"bf{k}-", [f"bx{k}-"], q.at[lo:hi, 1, e:BLK], q.at[lo:hi, 3, e:BLK], "x-")

    def cells_dot(lo, hi, rows):
        right = q[lo:hi].reshape((hi - lo) * 512, RANK)
        return jnp.dot(xd[rows, lo * 512:hi * 512], right, preferred_element_type=F32)

    def cells(lo, hi, rows):
        def run():
            part = cells_dot(lo, hi, rows)
            p[rows] = part if lo == 0 else p[rows] + part
        return run

    task("load", [], 0.1, loaded)
    for k, (lo, hi) in enumerate(GROUPS):
        task(f"x{k}", [f"x{k - 1}" if k else "load"], 0.4 * (hi - lo), lambda lo=lo, hi=hi: densify(lo, hi))
    for k, (lo, hi) in enumerate(GROUPS):
        came = [f"b{n}{k}{s}" for n in "xf" for s in "+-"] + (
            [f"z{n}{k}{s}" for n in "onf" for s in "+-"] if k else ["ax+", "ax-", "af+", "af-"])
        if k < 4:
            for i in range(4):
                task(f"c{k}.{i}", [f"x{k}"] + came + ([f"c{k - 1}.{i}"] if k else []), 0.3 * (hi - lo),
                     cells(lo, hi, slice(i * 512, (i + 1) * 512)))
        else:
            for i in range(8):
                task(f"c4.{i}", ["x4", f"c3.{i // 2}"] + came, 0.15, cells(lo, hi, slice(i * CHUNK, (i + 1) * CHUNK)))

    def lanes(i):
        return slice(i * CHUNK, (i + 1) * CHUNK)

    def add(rows, other):
        def run():
            p[rows] = p[rows] + other[...]
        return run

    lows = [slice((4 + i) * CHUNK, (4 + i) * CHUNK + HALF) for i in range(4)]
    highs = [slice((4 + i) * CHUNK + HALF, (5 + i) * CHUNK) for i in range(4)]
    for i in range(4):
        send(f"pair{i}", [f"c4.{i}"], p.at[lanes(i)], pcr.at[i], "c")
        task(f"own{i}", [f"c4.{4 + i}", f"pair{i}"], 0.1, add(lanes(4 + i), pcr.at[i]))
    send("yh+", ["own0"], p.at[lows[0]], yr.at[0], "y+")
    send("yh-", ["own0"], p.at[highs[0]], yr.at[1], "y-")
    send("ys+", ["own1"], p.at[highs[1]], yr.at[2], "y+")
    send("ys-", ["own2"], p.at[lows[2]], yr.at[3], "y-")
    send("yf+", ["own1", "yh+"], p.at[lows[1]], yr.at[4], "y+", add(lows[1], yr.at[0]), 0.05)
    send("yf-", ["own2", "yh-"], p.at[highs[2]], yr.at[5], "y-", add(highs[2], yr.at[1]), 0.05)

    def rounded():
        low = p[lows[3]] + yr[3] + yr[4]
        high = p[highs[3]] + yr[2] + yr[5]
        cbt[:, lanes(7)] = jnp.concatenate([low, high], axis=0).T.astype(BF)

    task("cb", ["own3", "ys+", "ys-", "yf+", "yf-"], 0.3, rounded)
    up, down = slice(0, RANK // 2), slice(RANK // 2, RANK)
    send("g+", ["cb"], cbt.at[:, lanes(7)], cbt.at[:, lanes(6)], "y+")
    send("g-", ["cb"], cbt.at[:, lanes(7)], cbt.at[:, lanes(5)], "y-")
    send("k3", ["cb"], cbt.at[:, lanes(7)], cbt.at[:, lanes(3)], "c")
    send("k+", ["g+"], cbt.at[up, lanes(6)], cbt.at[up, lanes(4)], "y+")
    send("k-", ["g-"], cbt.at[down, lanes(5)], cbt.at[down, lanes(4)], "y-")
    send("k2", ["g+"], cbt.at[:, lanes(6)], cbt.at[:, lanes(2)], "c")
    send("k1", ["g-"], cbt.at[:, lanes(5)], cbt.at[:, lanes(1)], "c")
    send("k0", ["k+", "k-"], cbt.at[:, lanes(4)], cbt.at[:, lanes(0)], "c")

    def genes(n, i):
        def run():
            cols = slice((2 * n + i) * 256, (2 * n + i + 1) * 256)
            zt[n, i] = jnp.dot(cbt[...], xd[:, cols], preferred_element_type=F32)
        return run

    for n in range(8):
        for i in range(2):
            task(f"z{n}.{i}", ["cb", "g+", "g-", "k+", "k-", "k0", "k1", "k2", "k3"], 0.6, genes(n, i))

    SPOT = {0: (0, 0), 1: (0, 1), -1: (1, 0), 2: (1, 1)}

    def part(n, rows, dx):
        i, j = SPOT[dx]
        return zt[n, i, rows, j * BLK:(j + 1) * BLK]

    SLOT = {2: 0, 1: 1, -1: 2, 0: 3}
    cut = RA // 2
    a1, a2 = slice(0, cut), slice(cut, RA)
    tops = slice(0, RA)

    def a_z(label, pieces):
        for d in range(4, 0, -1):
            for i, (s, sign) in enumerate(SIGNS):
                if d == 4 and len(pieces) == 1:
                    spots, rows = pieces, (a1, a2)[i]
                else:
                    spots, rows = (pieces if d < 4 else pieces[i:i + 1]), tops
                n = ORDER[sign * d]

                def run(d=d, i=i, n=n, spots=spots, rows=rows):
                    for dx in spots:
                        value = part(n, rows, dx)
                        if d < 3 or d == 3 and len(pieces) == 2 and dx == pieces[i]:
                            value = value + azr[i, d, SLOT[dx], rows].astype(F32)
                        elif d == 3 and len(pieces) == 1:
                            mine = (a1, a2)[i]
                            got = azr[i, 3, SLOT[dx], mine].astype(F32)
                            fill = jnp.zeros_like(got)
                            value = value + jnp.concatenate([got, fill] if i == 0 else [fill, got], axis=0)
                        azs[i, d - 1, SLOT[dx], rows] = value.astype(BF)

                m = slice(SLOT[spots[0]], SLOT[spots[-1]] + 1)
                tiles_of = {f"z{n}.{SPOT[dx][0]}" for dx in spots}
                send(f"{label}{d}{s}", sorted(tiles_of) + ([f"{label}{d + 1}{s}"] if d < 4 else []),
                     azs.at[i, d - 1, m, rows], azr.at[i, d - 1, m, rows], "z" + s, run, 0.08 * len(spots))

    a_z("af", [2])
    a_z("an", [1, -1])
    a_z("ao", [0])

    def a_sum(pieces):
        def run():
            for dx in pieces:
                za[SLOT[dx]] = part(0, tops, dx) + azr[0, 0, SLOT[dx]].astype(F32) + azr[1, 0, SLOT[dx]].astype(F32)
        return run

    task("asf", ["z0.1", "af1+", "af1-"], 0.08, a_sum([2]))
    task("asn", ["z0.0", "z0.1", "an1+", "an1-"], 0.15, a_sum([1, -1]))
    task("aso", ["z0.0", "ao1+", "ao1-"], 0.08, a_sum([0]))

    def a_add(spot, rows, n):
        def run():
            za[spot, rows] = za[spot, rows] + axr[n]
        return run

    send("a0", ["asf"], za.at[0, a1], axr.at[0], "x+")
    send("a1", ["asf"], za.at[0, a2], axr.at[1], "x-")
    send("a2", ["asn"], za.at[1, a2], axr.at[2], "x+")
    send("a3", ["asn"], za.at[2, a1], axr.at[3], "x-")
    send("a4", ["asn", "a0"], za.at[1, a1], axr.at[4], "x+", a_add(1, a1, 0), 0.05)
    send("a5", ["asn", "a1"], za.at[2, a2], axr.at[5], "x-", a_add(2, a2, 1), 0.05)

    b1, b2 = slice(RA, RA + RB1), slice(RA + RB1, RANK)
    v1, v2, v = slice(0, RB1), slice(RB1, RB), slice(0, RB)

    KINDS = ((2, b1, None), (2, b2, None), (1, b2, None), (-1, b1, None), (1, b1, 0), (-1, b2, 1))

    def b_x(kind, k):
        lo, hi = GROUPS[k]
        dx, rows, first = KINDS[kind]

        def run():
            for n in range(lo, hi):
                value = part(n, rows, dx)
                if first is not None:
                    value = value + br[first, n].astype(F32)
                bs[kind, n] = value.astype(BF)

        send(f"b{kind}.{k}", [f"z{n}.{SPOT[dx][0]}" for n in range(lo, hi)] + (
            [] if first is None else [f"b{first}.{k}"]), bs.at[kind, lo:hi], br.at[kind, lo:hi],
            "x-" if kind % 2 else "x+", run, 0.07 * (hi - lo))

    def b_total(k):
        lo, hi = GROUPS[k]

        def run():
            for n in range(lo, hi):
                zb[n, v1] = part(n, b1, 0) + br[3, n].astype(F32) + br[4, n].astype(F32)
                zb[n, v2] = part(n, b2, 0) + br[2, n].astype(F32) + br[5, n].astype(F32)
        task(f"bt{k}", [f"z{n}.0" for n in range(lo, hi)] + [f"b{i}.{k}" for i in range(2, 6)],
             0.12 * (hi - lo), run)

    for k in range(5):
        for kind in range(6):
            b_x(kind, k)
        b_total(k)
    for d in range(4, 0, -1):
        for i, (s, sign) in enumerate(SIGNS):
            n = ORDER[sign * d]
            rows = (v1, v2)[i] if d == 4 else v
            came = (v1, v2)[i] if d == 3 else v

            def run(n=n, i=i, d=d, came=came):
                if d < 4:
                    zb[n, came] = zb[n, came] + bzr[i, d, came]
            send(f"bz{d}{s}", [f"bt{d}"] + ([f"bz{d + 1}{s}"] if d < 4 else []),
                 zb.at[n, rows], bzr.at[i, d - 1, rows], "z" + s, run, 0.05)

    def result():
        top = jnp.concatenate([za[3, a1] + axr[3] + axr[4], za[3, a2] + axr[2] + axr[5]], axis=0)
        bottom = zb[0] + bzr[0, 0] + bzr[1, 0]
        out[...] = jnp.concatenate([top, bottom], axis=0).T

    task("out", ["aso", "a2", "a3", "a4", "a5", "bt0", "bz1+", "bz1-"], 0.3, result)
    plan.run()


def local(block_tiles, block_coords, block_counts, basis_rows):
    vmem = pl.BlockSpec(memory_space=pltpu.VMEM)
    return pl.pallas_call(
        kernel,
        out_shape=jax.ShapeDtypeStruct((BLK, RANK), F32),
        in_specs=[vmem, vmem, pl.BlockSpec(memory_space=pl.ANY), vmem],
        out_specs=vmem,
        scratch_shapes=[
            pltpu.VMEM((SLOTS + 1, BLK, BLK), BF),
            pltpu.VMEM((ROWS, COLS), BF),
            pltpu.VMEM((NZ, NX, BLK, RANK), BF),
            pltpu.VMEM((ROWS, RANK), F32),
            pltpu.VMEM((4, CHUNK, RANK), F32),
            pltpu.VMEM((6, CHUNK // 2, RANK), F32),
            pltpu.VMEM((RANK, ROWS), BF),
            pltpu.VMEM((NZ, 2, RANK, 256), F32),
            pltpu.VMEM((4, RA, BLK), F32),
            pltpu.VMEM((NZ, RB, BLK), F32),
            pltpu.VMEM((2, 4, 4, RA, BLK), BF),
            pltpu.VMEM((2, 4, 4, RA, BLK), BF),
            pltpu.VMEM((6, RA // 2, BLK), F32),
            pltpu.VMEM((6, NZ, RB1, BLK), BF),
            pltpu.VMEM((6, NZ, RB1, BLK), BF),
            pltpu.VMEM((2, 4, RB, BLK), F32),
            pltpu.VMEM((1, 512), jnp.int32),
            pltpu.SMEM((1, 512), jnp.int32),
            pltpu.SemaphoreType.DMA((N_SEM,)),
            pltpu.SemaphoreType.DMA((N_SEM,)),
            pltpu.SemaphoreType.DMA((8,)),
            pltpu.SemaphoreType.DMA,
        ],
        compiler_params=pltpu.CompilerParams(
            collective_id=0, has_side_effects=True, vmem_limit_bytes=60 * 1024 * 1024),
        cost_estimate=pl.CostEstimate(flops=4 * ROWS * COLS * RANK, bytes_accessed=11_000_000,
                                      transcendentals=0),
    )(block_counts, block_coords.T, block_tiles, basis_rows)


def solution(mesh):
    return jax.shard_map(
        local,
        mesh=mesh,
        in_specs=(
            P("cells", "genes", None),
            P("cells", "genes"),
            P("cells", "genes"),
            P(("cells", "genes"), None),
        ),
        out_specs=P(("cells", "genes"), None),
        check_vma=False,
    )
```

time: 697 us -> 88 us (0.13)
  waiting for transfers between devices: 306 us -> 0 us
  other arithmetic: 197 us -> 0 us
  Pallas kernels: 0 us -> 85.7 us
  matrix products: 79.4 us -> 0 us
  local copies, waits for them, and re-layouts: 50.7 us -> 1.57 us
  blocking collectives: 48.9 us -> 0 us
  between operations: 13.4 us -> 0.66 us
    reduce_scatter x1 -> x0, waiting for transfers between devices: 222 us -> none  [local(): return lax.psum_scatter(gene_flat, 'cells', scatter_dimension=0, tiled=True)]
    scatter-add x16 -> x0, other arithmetic: 185 us -> none  [the longest x8 112 us: gene_turn(): return running.at[genes_here].add(product)]
    pallas_call x0 -> x1, Pallas kernels: none -> 85.7 us  [local(): pl.pallas_call(kernel, out_shape=jax.ShapeDtypeStruct((BLK, RANK), F32),...]
    all_gather x1 -> x0, waiting for transfers between devices: 82.6 us -> none  [local(): gathered = lax.all_gather(basis_rows, 'cells', axis=0, tiled=True)]
    dot_general x16 -> x0, matrix products: 79.4 us -> none  [the longest x8 42.3 us: cell_turn(): jnp.einsum('sab,sbk->sak', piece, chosen, preferred_element_type=jnp.floa...]
    psum x1 -> x0, blocking collectives: 48.9 us -> none  [local(): cell_basis = lax.psum(row_flat, 'genes').astype(jnp.bfloat16)]
    gather x16 -> x0, local copies, waits for them, and re-layouts: 47.3 us -> none  [the longest x8 31.7 us: cell_turn(): chosen = basis_blocks[genes_here]]
    lt x16 -> x0, other arithmetic: 10.4 us -> none  [drop_dead(): live = first_slot + jnp.arange(group_size) < live_count]
  transfers between devices with their start and end apart: 2 -> 0, of which waited for: 2 -> 0; matrix products, arithmetic and copies ran while one was open for 0% -> 0% of each run, Pallas kernels for 0% -> 0%
where the time goes in v4:
time: 88 us; the launch traced here: 87.9 us
  Pallas kernels  85.7 us (97%)
  local copies, waits for them, and re-layouts  1.57 us (2%)
    pallas_call x1, Pallas kernels, local(): pl.pallas_call(kernel, out_shape=jax.ShapeDtypeStruct((BLK, RANK), F32),...  85.7 us

profile of v4, /device:TPU:8, one launch (start us, length us, event | category | flops | bytes accessed | tf_op | source)
XLA Modules:
  0.0 87.9 jit_solution(12985008229808241968)
XLA Ops:
  0.7 85.7 %shard_map.46 = f32[128,256]{1,0:T(8,128)} custom-call(s32[1,1]{1,0:T(1,128)S(6)} %copy.6.count_ref, s32[2,320]{1,0:T(2,128)} %bitcast.1, bf16[320,128,128]{2,1,0:T(8,128)(2,1)} %tiles_hbm.1, bf16[128,256]{1,0:T(8,128)(2,1)} %basis.1), custom_call_target="tpu_custom_call" | custom-call | flops 8589934592 | bytes 11000000 | tf_op jit(solution)/shard_map/pallas_call | solution.py:389
  86.3 1.6 %copy.7 = f32[128,256]{1,0:T(8,128)} copy(f32[128,256]{1,0:T(8,128)} %shard_map.46) | data formatting | bytes 262144

commit v5 on v4

--- a/solution.py
+++ b/solution.py
@@ -30,7 +30,23 @@
 HOP = 1.5
 LINK = {"x+": 50e3, "x-": 50e3, "z+": 50e3, "z-": 50e3, "y+": 50e3, "y-": 50e3, "c": 500e3}
 ISSUE = 0.08
-N_SEM = 136
+C_A, C_B, C_P = 0.04, 0.035, 0.1
+N_SEM = 150
+HEAD = 16
+
+
+def pack(value):
+    top = jnp.max(jnp.abs(value), axis=0, keepdims=True)
+    power = jnp.floor(jnp.log2(jnp.maximum(top, 1e-30))) + 1.0
+    whole = jnp.clip(jnp.round(value * jnp.exp2(15.0 - power)), -32767.0, 32767.0)
+    both = jnp.concatenate([whole, jnp.broadcast_to(power, (HEAD, value.shape[1]))], axis=0)
+    return both.astype(jnp.int32).astype(jnp.int16)
+
+
+def unpack(packed):
+    value = packed.astype(jnp.int32).astype(F32)
+    rows = value.shape[0] - HEAD
+    return value[:rows] * jnp.exp2(value[rows:rows + 1] - 15.0)
 
 
 class Plan:
@@ -106,8 +122,8 @@
                 self.tasks[name][3][0].wait_send()
 
 
-def kernel(count_ref, coords, tiles_hbm, basis, out, tiles, xd, q, p, pcr, yr, cbt, zt,
-           za, zb, azs, azr, axr, bs, br, bzr, slot_v, slot_ref, ssem, rsem, tsem, slot_sem):
+def kernel(count_ref, coords, tiles_hbm, basis, out, tiles, xd, q, p, pcr, ys, yr, cbt, zt,
+           za, zb, azs, azr, axr, axr2, bs, br, bzs, bzr, slot_v, slot_ref, ssem, rsem, tsem, slot_sem):
     c = lax.axis_index("cells")
     g = lax.axis_index("genes")
     z, x = c // NX, c % NX
@@ -142,8 +158,9 @@
     b, k = coords[0:1, :], coords[1:2, :]
     chunk = lax.shift_right_logical(b, 1)
     dy = ((chunk & 3) - y) & 3
-    dy = jnp.where(dy == 0, 3, jnp.where(dy == 3, 2, 2 - dy))
-    pos = jnp.where(lax.shift_right_logical(chunk, 2) == core, 4, 0) + dy
+    own = lax.shift_right_logical(chunk, 2) == core
+    pos = jnp.where(own, jnp.where(dy == 0, 0, jnp.where(dy == 3, 2, jnp.where(dy == 1, 3, 6))),
+                    jnp.where(dy == 0, 1, jnp.where(dy == 3, 4, jnp.where(dy == 1, 5, 7))))
     dz = (lax.shift_right_logical(k, 2) - z) & 7
     dz = jnp.where(dz == 0, 0, jnp.where(dz <= 3, 2 * dz - 1, jnp.where(dz == 4, 7, 2 * (NZ - dz))))
     dx = ((k & 3) - x) & 3
@@ -228,43 +245,56 @@
             p[rows] = p[rows] + other[...]
         return run
 
-    lows = [slice((4 + i) * CHUNK, (4 + i) * CHUNK + HALF) for i in range(4)]
-    highs = [slice((4 + i) * CHUNK + HALF, (5 + i) * CHUNK) for i in range(4)]
-    for i in range(4):
-        send(f"pair{i}", [f"c4.{i}"], p.at[lanes(i)], pcr.at[i], "c")
-        task(f"own{i}", [f"c4.{4 + i}", f"pair{i}"], 0.1, add(lanes(4 + i), pcr.at[i]))
-    send("yh+", ["own0"], p.at[lows[0]], yr.at[0], "y+")
-    send("yh-", ["own0"], p.at[highs[0]], yr.at[1], "y-")
-    send("ys+", ["own1"], p.at[highs[1]], yr.at[2], "y+")
-    send("ys-", ["own2"], p.at[lows[2]], yr.at[3], "y-")
-    send("yf+", ["own1", "yh+"], p.at[lows[1]], yr.at[4], "y+", add(lows[1], yr.at[0]), 0.05)
-    send("yf-", ["own2", "yh-"], p.at[highs[2]], yr.at[5], "y-", add(highs[2], yr.at[1]), 0.05)
+    OWN, OTHER = {0: 0, -1: 2, 1: 3, 2: 6}, {0: 1, -1: 4, 1: 5, 2: 7}
+    low = {dy: slice(i * CHUNK, i * CHUNK + HALF) for dy, i in OWN.items()}
+    high = {dy: slice(i * CHUNK + HALF, (i + 1) * CHUNK) for dy, i in OWN.items()}
+    for dy in (2, 1, -1, 0):
+        send(f"pair{dy}", [f"c4.{OTHER[dy]}"], p.at[lanes(OTHER[dy])], pcr.at[dy + 1], "c")
+        task(f"own{dy}", [f"c4.{OWN[dy]}", f"pair{dy}"], 0.1, add(lanes(OWN[dy]), pcr.at[dy + 1]))
+
+    def y_send(n, needs, rows, to, first=None):
+        def run():
+            ys[n] = pack(p[rows] if first is None else p[rows] + unpack(yr[first]))
+        send(f"y{n}", needs, ys.at[n], yr.at[n], to, run, 0.15)
+
+    y_send(0, ["own2"], low[2], "y+")
+    y_send(1, ["own2"], high[2], "y-")
+    y_send(2, ["own1"], high[1], "y+")
+    y_send(3, ["own-1"], low[-1], "y-")
+    y_send(4, ["own1", "y0"], low[1], "y+", 0)
+    y_send(5, ["own-1", "y1"], high[-1], "y-", 1)
 
     def rounded():
-        low = p[lows[3]] + yr[3] + yr[4]
-        high = p[highs[3]] + yr[2] + yr[5]
-        cbt[:, lanes(7)] = jnp.concatenate([low, high], axis=0).T.astype(BF)
-
-    task("cb", ["own3", "ys+", "ys-", "yf+", "yf-"], 0.3, rounded)
+        top = p[low[0]] + unpack(yr[3]) + unpack(yr[4])
+        bottom = p[high[0]] + unpack(yr[2]) + unpack(yr[5])
+        cbt[:, lanes(0)] = jnp.concatenate([top, bottom], axis=0).T.astype(BF)
+
+    task("cb", ["own0", "y2", "y3", "y4", "y5"], 0.4, rounded)
     up, down = slice(0, RANK // 2), slice(RANK // 2, RANK)
-    send("g+", ["cb"], cbt.at[:, lanes(7)], cbt.at[:, lanes(6)], "y+")
-    send("g-", ["cb"], cbt.at[:, lanes(7)], cbt.at[:, lanes(5)], "y-")
-    send("k3", ["cb"], cbt.at[:, lanes(7)], cbt.at[:, lanes(3)], "c")
-    send("k+", ["g+"], cbt.at[up, lanes(6)], cbt.at[up, lanes(4)], "y+")
-    send("k-", ["g-"], cbt.at[down, lanes(5)], cbt.at[down, lanes(4)], "y-")
-    send("k2", ["g+"], cbt.at[:, lanes(6)], cbt.at[:, lanes(2)], "c")
-    send("k1", ["g-"], cbt.at[:, lanes(5)], cbt.at[:, lanes(1)], "c")
-    send("k0", ["k+", "k-"], cbt.at[:, lanes(4)], cbt.at[:, lanes(0)], "c")
-
-    def genes(n, i):
+    for half, rows in (("u", up), ("d", down)):
+        send(f"g+{half}", ["cb"], cbt.at[rows, lanes(0)], cbt.at[rows, lanes(2)], "y+")
+        send(f"g-{half}", ["cb"], cbt.at[rows, lanes(0)], cbt.at[rows, lanes(3)], "y-")
+    send("k0", ["cb"], cbt.at[:, lanes(0)], cbt.at[:, lanes(1)], "c")
+    send("k+", ["g+u"], cbt.at[up, lanes(2)], cbt.at[up, lanes(6)], "y+")
+    send("k-", ["g-d"], cbt.at[down, lanes(3)], cbt.at[down, lanes(6)], "y-")
+    send("k1", ["g+u", "g+d"], cbt.at[:, lanes(2)], cbt.at[:, lanes(4)], "c")
+    send("k2", ["g-u", "g-d"], cbt.at[:, lanes(3)], cbt.at[:, lanes(5)], "c")
+    send("k3", ["k+", "k-"], cbt.at[:, lanes(6)], cbt.at[:, lanes(7)], "c")
+
+    def genes(n, i, lo, hi):
         def run():
             cols = slice((2 * n + i) * 256, (2 * n + i + 1) * 256)
-            zt[n, i] = jnp.dot(cbt[...], xd[:, cols], preferred_element_type=F32)
+            rows = slice(lo * CHUNK, hi * CHUNK)
+            part = jnp.dot(cbt[:, rows], xd[rows, cols], preferred_element_type=F32)
+            zt[n, i] = part if lo == 0 else zt[n, i] + part
         return run
 
     for n in range(8):
         for i in range(2):
-            task(f"z{n}.{i}", ["cb", "g+", "g-", "k+", "k-", "k0", "k1", "k2", "k3"], 0.6, genes(n, i))
+            task(f"t{n}.{i}", ["cb", "k0"], 0.17, genes(n, i, 0, 2))
+            task(f"u{n}.{i}", [f"t{n}.{i}", "g+u", "g+d", "g-u", "g-d"], 0.2, genes(n, i, 2, 4))
+            task(f"v{n}.{i}", [f"u{n}.{i}", "k1", "k2"], 0.2, genes(n, i, 4, 6))
+            task(f"z{n}.{i}", [f"v{n}.{i}", "k+", "k-", "k3"], 0.2, genes(n, i, 6, 8))
 
     SPOT = {0: (0, 0), 1: (0, 1), -1: (1, 0), 2: (1, 1)}
 
@@ -272,28 +302,24 @@
         i, j = SPOT[dx]
         return zt[n, i, rows, j * BLK:(j + 1) * BLK]
 
-    SLOT = {2: 0, 1: 1, -1: 2, 0: 3}
+    SLOT = {2: 0, -1: 1, 1: 2, 0: 3}
     cut = RA // 2
     a1, a2 = slice(0, cut), slice(cut, RA)
     tops = slice(0, RA)
 
-    def a_z(label, pieces):
+    def a_z(label, pieces, far):
         for d in range(4, 0, -1):
             for i, (s, sign) in enumerate(SIGNS):
-                if d == 4 and len(pieces) == 1:
-                    spots, rows = pieces, (a1, a2)[i]
-                else:
-                    spots, rows = (pieces if d < 4 else pieces[i:i + 1]), tops
+                spots, rows = far[i] if d == 4 else (pieces, tops)
                 n = ORDER[sign * d]
 
                 def run(d=d, i=i, n=n, spots=spots, rows=rows):
                     for dx in spots:
                         value = part(n, rows, dx)
-                        if d < 3 or d == 3 and len(pieces) == 2 and dx == pieces[i]:
+                        if d < 3 or d == 3 and far[i][1] == tops and dx in far[i][0]:
                             value = value + azr[i, d, SLOT[dx], rows].astype(F32)
-                        elif d == 3 and len(pieces) == 1:
-                            mine = (a1, a2)[i]
-                            got = azr[i, 3, SLOT[dx], mine].astype(F32)
+                        elif d == 3 and far[i][1] != tops:
+                            got = azr[i, 3, SLOT[dx], far[i][1]].astype(F32)
                             fill = jnp.zeros_like(got)
                             value = value + jnp.concatenate([got, fill] if i == 0 else [fill, got], axis=0)
                         azs[i, d - 1, SLOT[dx], rows] = value.astype(BF)
@@ -301,11 +327,10 @@
                 m = slice(SLOT[spots[0]], SLOT[spots[-1]] + 1)
                 tiles_of = {f"z{n}.{SPOT[dx][0]}" for dx in spots}
                 send(f"{label}{d}{s}", sorted(tiles_of) + ([f"{label}{d + 1}{s}"] if d < 4 else []),
-                     azs.at[i, d - 1, m, rows], azr.at[i, d - 1, m, rows], "z" + s, run, 0.08 * len(spots))
-
-    a_z("af", [2])
-    a_z("an", [1, -1])
-    a_z("ao", [0])
+                     azs.at[i, d - 1, m, rows], azr.at[i, d - 1, m, rows], "z" + s, run, C_A * len(spots))
+
+    a_z("af", (2,), (((2,), a1), ((2,), a2)))
+    a_z("an", (-1, 1, 0), (((1, 0), tops), ((-1,), tops)))
 
     def a_sum(pieces):
         def run():
@@ -313,9 +338,8 @@
                 za[SLOT[dx]] = part(0, tops, dx) + azr[0, 0, SLOT[dx]].astype(F32) + azr[1, 0, SLOT[dx]].astype(F32)
         return run
 
-    task("asf", ["z0.1", "af1+", "af1-"], 0.08, a_sum([2]))
-    task("asn", ["z0.0", "z0.1", "an1+", "an1-"], 0.15, a_sum([1, -1]))
-    task("aso", ["z0.0", "ao1+", "ao1-"], 0.08, a_sum([0]))
+    task("asf", ["z0.1", "af1+", "af1-"], C_A, a_sum([2]))
+    task("asn", ["z0.0", "z0.1", "an1+", "an1-"], 3 * C_A, a_sum([-1, 1, 0]))
 
     def a_add(spot, rows, n):
         def run():
@@ -324,63 +348,68 @@
 
     send("a0", ["asf"], za.at[0, a1], axr.at[0], "x+")
     send("a1", ["asf"], za.at[0, a2], axr.at[1], "x-")
-    send("a2", ["asn"], za.at[1, a2], axr.at[2], "x+")
-    send("a3", ["asn"], za.at[2, a1], axr.at[3], "x-")
-    send("a4", ["asn", "a0"], za.at[1, a1], axr.at[4], "x+", a_add(1, a1, 0), 0.05)
-    send("a5", ["asn", "a1"], za.at[2, a2], axr.at[5], "x-", a_add(2, a2, 1), 0.05)
+    send("a2", ["asn", "a0"], za.at[2], axr2.at[0], "x+", a_add(2, a1, 0), 0.05)
+    send("a3", ["asn", "a1"], za.at[1], axr2.at[1], "x-", a_add(1, a2, 1), 0.05)
 
     b1, b2 = slice(RA, RA + RB1), slice(RA + RB1, RANK)
     v1, v2, v = slice(0, RB1), slice(RB1, RB), slice(0, RB)
 
-    KINDS = ((2, b1, None), (2, b2, None), (1, b2, None), (-1, b1, None), (1, b1, 0), (-1, b2, 1))
-
-    def b_x(kind, k):
+    KINDS = ((2, b1, None), (2, b2, None), (1, b1, 0), (1, b2, None), (-1, b1, None), (-1, b2, 1))
+
+    def b_x(name, kinds, k, to):
         lo, hi = GROUPS[k]
-        dx, rows, first = KINDS[kind]
-
-        def run():
-            for n in range(lo, hi):
-                value = part(n, rows, dx)
-                if first is not None:
-                    value = value + br[first, n].astype(F32)
-                bs[kind, n] = value.astype(BF)
-
-        send(f"b{kind}.{k}", [f"z{n}.{SPOT[dx][0]}" for n in range(lo, hi)] + (
-            [] if first is None else [f"b{first}.{k}"]), bs.at[kind, lo:hi], br.at[kind, lo:hi],
-            "x-" if kind % 2 else "x+", run, 0.07 * (hi - lo))
+        needs = set()
+        for kind in kinds:
+            dx, _, first = KINDS[kind]
+            needs |= {f"z{n}.{SPOT[dx][0]}" for n in range(lo, hi)}
+            if first is not None:
+                needs.add(f"bh{first}.{k}")
+
+        def run():
+            for kind in kinds:
+                dx, rows, first = KINDS[kind]
+                for n in range(lo, hi):
+                    value = part(n, rows, dx)
+                    if first is not None:
+                        value = value + br[first, n].astype(F32)
+                    bs[kind, n] = value.astype(BF)
+
+        m = slice(kinds[0], kinds[-1] + 1)
+        send(f"{name}.{k}", sorted(needs), bs.at[m, lo:hi], br.at[m, lo:hi], to, run, C_B * len(kinds) * (hi - lo))
 
     def b_total(k):
         lo, hi = GROUPS[k]
 
         def run():
             for n in range(lo, hi):
-                zb[n, v1] = part(n, b1, 0) + br[3, n].astype(F32) + br[4, n].astype(F32)
-                zb[n, v2] = part(n, b2, 0) + br[2, n].astype(F32) + br[5, n].astype(F32)
-        task(f"bt{k}", [f"z{n}.0" for n in range(lo, hi)] + [f"b{i}.{k}" for i in range(2, 6)],
-             0.12 * (hi - lo), run)
+                zb[n, v1] = part(n, b1, 0) + br[2, n].astype(F32) + br[4, n].astype(F32)
+                zb[n, v2] = part(n, b2, 0) + br[3, n].astype(F32) + br[5, n].astype(F32)
+        task(f"bt{k}", [f"z{n}.0" for n in range(lo, hi)] + [f"bf0.{k}", f"bf1.{k}"], 3 * C_B * (hi - lo), run)
 
     for k in range(5):
-        for kind in range(6):
-            b_x(kind, k)
+        b_x("bh0", (0,), k, "x+")
+        b_x("bh1", (1,), k, "x-")
+        b_x("bf0", (2, 3), k, "x+")
+        b_x("bf1", (4, 5), k, "x-")
         b_total(k)
     for d in range(4, 0, -1):
         for i, (s, sign) in enumerate(SIGNS):
-            n = ORDER[sign * d]
-            rows = (v1, v2)[i] if d == 4 else v
-            came = (v1, v2)[i] if d == 3 else v
-
-            def run(n=n, i=i, d=d, came=came):
-                if d < 4:
-                    zb[n, came] = zb[n, came] + bzr[i, d, came]
-            send(f"bz{d}{s}", [f"bt{d}"] + ([f"bz{d + 1}{s}"] if d < 4 else []),
-                 zb.at[n, rows], bzr.at[i, d - 1, rows], "z" + s, run, 0.05)
+            for j, rows in enumerate((v1, v2)):
+                if d == 4 and i != j:
+                    continue
+                first = d == 4 or d == 3 and i != j
+
+                def run(n=ORDER[sign * d], i=i, j=j, d=d, rows=rows, first=first):
+                    bzs[i, d - 1, j] = pack(zb[n, rows] if first else zb[n, rows] + unpack(bzr[i, d, j]))
+                send(f"bz{d}{s}{j}", [f"bt{d}"] + ([] if first else [f"bz{d + 1}{s}{j}"]),
+                     bzs.at[i, d - 1, j], bzr.at[i, d - 1, j], "z" + s, run, C_P)
 
     def result():
-        top = jnp.concatenate([za[3, a1] + axr[3] + axr[4], za[3, a2] + axr[2] + axr[5]], axis=0)
-        bottom = zb[0] + bzr[0, 0] + bzr[1, 0]
-        out[...] = jnp.concatenate([top, bottom], axis=0).T
-
-    task("out", ["aso", "a2", "a3", "a4", "a5", "bt0", "bz1+", "bz1-"], 0.3, result)
+        top = za[3] + axr2[0] + axr2[1]
+        bottom = [zb[0, rows] + unpack(bzr[0, 0, j]) + unpack(bzr[1, 0, j]) for j, rows in enumerate((v1, v2))]
+        out[...] = jnp.concatenate([top] + bottom, axis=0).T
+
+    task("out", ["asn", "a2", "a3", "bt0", "bz1+0", "bz1+1", "bz1-0", "bz1-1"], 0.3, result)
     plan.run()
 
 
@@ -397,17 +426,20 @@
             pltpu.VMEM((NZ, NX, BLK, RANK), BF),
             pltpu.VMEM((ROWS, RANK), F32),
             pltpu.VMEM((4, CHUNK, RANK), F32),
-            pltpu.VMEM((6, CHUNK // 2, RANK), F32),
+            pltpu.VMEM((6, HALF + HEAD, RANK), jnp.int16),
+            pltpu.VMEM((6, HALF + HEAD, RANK), jnp.int16),
             pltpu.VMEM((RANK, ROWS), BF),
             pltpu.VMEM((NZ, 2, RANK, 256), F32),
             pltpu.VMEM((4, RA, BLK), F32),
             pltpu.VMEM((NZ, RB, BLK), F32),
             pltpu.VMEM((2, 4, 4, RA, BLK), BF),
             pltpu.VMEM((2, 4, 4, RA, BLK), BF),
-            pltpu.VMEM((6, RA // 2, BLK), F32),
+            pltpu.VMEM((2, RA // 2, BLK), F32),
+            pltpu.VMEM((2, RA, BLK), F32),
             pltpu.VMEM((6, NZ, RB1, BLK), BF),
             pltpu.VMEM((6, NZ, RB1, BLK), BF),
-            pltpu.VMEM((2, 4, RB, BLK), F32),
+            pltpu.VMEM((2, 4, 2, RB1 + HEAD, BLK), jnp.int16),
+            pltpu.VMEM((2, 4, 2, RB1 + HEAD, BLK), jnp.int16),
             pltpu.VMEM((1, 512), jnp.int32),
             pltpu.SMEM((1, 512), jnp.int32),
             pltpu.SemaphoreType.DMA((N_SEM,)),

time: 88 us -> 83 us (0.943)
  Pallas kernels: 85.7 us -> 80.6 us
    pallas_call x1, Pallas kernels: 85.7 us -> 80.6 us  [local(): pl.pallas_call(kernel, out_shape=jax.ShapeDtypeStruct((BLK, RANK), F32),...]
where the time goes in v5:
time: 83 us; the launch traced here: 82.8 us
  Pallas kernels  80.6 us (97%)
  local copies, waits for them, and re-layouts  1.57 us (2%)
    pallas_call x1, Pallas kernels, local(): pl.pallas_call(kernel, out_shape=jax.ShapeDtypeStruct((BLK, RANK), F32),...  80.6 us

profile of v5, /device:TPU:8, one launch (start us, length us, event | category | flops | bytes accessed | tf_op | source)
XLA Modules:
  0.0 82.8 jit_solution(16937595294213337577)
XLA Ops:
  0.7 80.6 %shard_map.46 = f32[128,256]{1,0:T(8,128)} custom-call(s32[1,1]{1,0:T(1,128)S(6)} %copy.6.count_ref, s32[2,320]{1,0:T(2,128)} %bitcast.1, bf16[320,128,128]{2,1,0:T(8,128)(2,1)} %tiles_hbm.1, bf16[128,256]{1,0:T(8,128)(2,1)} %basis.1), custom_call_target="tpu_custom_call" | custom-call | flops 8589934592 | bytes 11000000 | tf_op jit(solution)/shard_map/pallas_call | solution.py:418
  81.3 1.6 %copy.7 = f32[128,256]{1,0:T(8,128)} copy(f32[128,256]{1,0:T(8,128)} %shard_map.46) | data formatting | bytes 262144

commit v6 on v5

--- a/solution.py
+++ b/solution.py
@@ -27,9 +27,10 @@
 GROUPS = ((0, 1), (1, 3), (3, 5), (5, 7), (7, 8))
 SIGNS = (("+", 1), ("-", -1))
 
-HOP = 1.5
+HOP = 1.6
 LINK = {"x+": 50e3, "x-": 50e3, "z+": 50e3, "z-": 50e3, "y+": 50e3, "y-": 50e3, "c": 500e3}
 ISSUE = 0.08
+LOADED = 5.0
 C_A, C_B, C_P = 0.04, 0.035, 0.1
 N_SEM = 150
 HEAD = 16
@@ -54,10 +55,12 @@
         self.ssem, self.rsem, self.where = ssem, rsem, where
         self.tasks = {}
         self.count = 0
-
-    def task(self, name, needs, cost, run, message=None):
+        self.after = {}
+
+    def task(self, name, needs, cost, run, message=None, after=0.0):
         assert name not in self.tasks, name
         self.tasks[name] = (tuple(needs), cost, run, message)
+        self.after[name] = after
 
     def send(self, name, needs, src, dst, to, run=None, cost=0.0):
         copy = pltpu.make_async_remote_copy(
@@ -86,7 +89,7 @@
         now, free, ready_at, order = 0.0, {}, {}, []
         left = dict.fromkeys(self.tasks)
         while left:
-            can = {n: max([ready_at[d] for d in self.tasks[n][0]], default=0.0)
+            can = {n: max([ready_at[d] for d in self.tasks[n][0]] + [self.after[n]])
                    for n in left if all(d in ready_at for d in self.tasks[n][0])}
             now = max(now, min(can.values()))
             name = max((n for n in can if can[n] <= now), key=lambda n: rank[n])
@@ -175,13 +178,13 @@
     to_smem.start()
     pl.semaphore_wait(barrier, len(where))
 
-    def densify(lo, hi):
+    def densify(n, i):
         def row(r, carry):
-            for col in range(lo * 4, hi * 4):
+            for col in range(n * 4, n * 4 + 4):
                 s = slot_ref[0, r * 32 + col]
                 xd[pl.ds(pl.multiple_of(r * BLK, BLK), BLK), col * BLK:(col + 1) * BLK] = tiles[s]
             return carry
-        lax.fori_loop(0, ROWS // BLK, row, 0)
+        lax.fori_loop(i * 4, i * 4 + 4, row, 0)
 
     def loaded():
         to_smem.wait()
@@ -223,19 +226,20 @@
             p[rows] = part if lo == 0 else p[rows] + part
         return run
 
-    task("load", [], 0.1, loaded)
-    for k, (lo, hi) in enumerate(GROUPS):
-        task(f"x{k}", [f"x{k - 1}" if k else "load"], 0.4 * (hi - lo), lambda lo=lo, hi=hi: densify(lo, hi))
+    task("load", [], 0.2, loaded, after=LOADED)
+    for n in range(NZ):
+        for i in range(4):
+            task(f"x{n}.{i}", ["load"], 0.15, lambda n=n, i=i: densify(n, i))
     for k, (lo, hi) in enumerate(GROUPS):
         came = [f"b{n}{k}{s}" for n in "xf" for s in "+-"] + (
             [f"z{n}{k}{s}" for n in "onf" for s in "+-"] if k else ["ax+", "ax-", "af+", "af-"])
         if k < 4:
             for i in range(4):
-                task(f"c{k}.{i}", [f"x{k}"] + came + ([f"c{k - 1}.{i}"] if k else []), 0.3 * (hi - lo),
+                task(f"c{k}.{i}", [f"x{n}.{i}" for n in range(lo, hi)] + came + ([f"c{k - 1}.{i}"] if k else []), 0.35 * (hi - lo),
                      cells(lo, hi, slice(i * 512, (i + 1) * 512)))
         else:
             for i in range(8):
-                task(f"c4.{i}", ["x4", f"c3.{i // 2}"] + came, 0.15, cells(lo, hi, slice(i * CHUNK, (i + 1) * CHUNK)))
+                task(f"c4.{i}", [f"x7.{i // 2}", f"c3.{i // 2}"] + came, 0.18, cells(lo, hi, slice(i * CHUNK, (i + 1) * CHUNK)))
 
     def lanes(i):
         return slice(i * CHUNK, (i + 1) * CHUNK)

time: 83 us -> 81.1 us (0.977)
  Pallas kernels: 80.6 us -> 78.7 us
    pallas_call x1, Pallas kernels: 80.6 us -> 78.7 us  [local(): pl.pallas_call(kernel, out_shape=jax.ShapeDtypeStruct((BLK, RANK), F32),...]
where the time goes in v6:
time: 81.1 us; the launch traced here: 81 us
  Pallas kernels  78.7 us (97%)
  local copies, waits for them, and re-layouts  1.57 us (2%)
    pallas_call x1, Pallas kernels, local(): pl.pallas_call(kernel, out_shape=jax.ShapeDtypeStruct((BLK, RANK), F32),...  78.7 us

profile of v6, /device:TPU:8, one launch (start us, length us, event | category | flops | bytes accessed | tf_op | source)
XLA Modules:
  0.0 81.0 jit_solution(8052318621596790595)
XLA Ops:
  0.7 78.7 %shard_map.46 = f32[128,256]{1,0:T(8,128)} custom-call(s32[1,1]{1,0:T(1,128)S(6)} %copy.6.count_ref, s32[2,320]{1,0:T(2,128)} %bitcast.1, bf16[320,128,128]{2,1,0:T(8,128)(2,1)} %tiles_hbm.1, bf16[128,256]{1,0:T(8,128)(2,1)} %basis.1), custom_call_target="tpu_custom_call" | custom-call | flops 8589934592 | bytes 11000000 | tf_op jit(solution)/shard_map/pallas_call | solution.py:422
  79.4 1.6 %copy.7 = f32[128,256]{1,0:T(8,128)} copy(f32[128,256]{1,0:T(8,128)} %shard_map.46) | data formatting | bytes 262144

commit v7 on v6

--- a/solution.py
+++ b/solution.py
@@ -125,8 +125,8 @@
                 self.tasks[name][3][0].wait_send()
 
 
-def kernel(count_ref, coords, tiles_hbm, basis, out, tiles, xd, q, p, pcr, ys, yr, cbt, zt,
-           za, zb, azs, azr, axr, axr2, bs, br, bzs, bzr, slot_v, slot_ref, ssem, rsem, tsem, slot_sem):
+def kernel(count_ref, coords, tiles_hbm, basis, out, tiles, q, p, pcr, ys, yr, cbt, zt,
+           za, zb, azs, azr, axr, axr2, bs, br, bzs, bzr, slot_v, slot_ref, ssem, rsem, tsem, slot_sem, basis_sem):
     c = lax.axis_index("cells")
     g = lax.axis_index("genes")
     z, x = c // NX, c % NX
@@ -149,42 +149,42 @@
     per = SLOTS // n_loads
     loads = [pltpu.make_async_copy(tiles_hbm.at[pl.ds(i * per, per)],
                                    tiles.at[pl.ds(i * per, per)], tsem.at[i]) for i in range(n_loads)]
+    own_basis = pltpu.make_async_copy(basis, q.at[0, 0], basis_sem)
+    own_basis.start()
     for load in loads:
         load.start()
-
     barrier = pltpu.get_barrier_semaphore()
     for to in where.values():
         pl.semaphore_signal(barrier, inc=1, device_id=to, device_id_type=MESH)
-    q[0, 0] = basis[...]
     tiles[SLOTS] = jnp.zeros((BLK, BLK), BF)
 
-    b, k = coords[0:1, :], coords[1:2, :]
-    chunk = lax.shift_right_logical(b, 1)
-    dy = ((chunk & 3) - y) & 3
-    own = lax.shift_right_logical(chunk, 2) == core
-    pos = jnp.where(own, jnp.where(dy == 0, 0, jnp.where(dy == 3, 2, jnp.where(dy == 1, 3, 6))),
-                    jnp.where(dy == 0, 1, jnp.where(dy == 3, 4, jnp.where(dy == 1, 5, 7))))
-    dz = (lax.shift_right_logical(k, 2) - z) & 7
-    dz = jnp.where(dz == 0, 0, jnp.where(dz <= 3, 2 * dz - 1, jnp.where(dz == 4, 7, 2 * (NZ - dz))))
-    dx = ((k & 3) - x) & 3
-    dx = jnp.where(dx >= 2, 5 - dx, dx)
-    place = (pos * 2 + (b & 1)) * 32 + dz * NX + dx
-    live = lax.broadcasted_iota(jnp.int32, (1, SLOTS), 1) < count_ref[...]
-    place = jnp.broadcast_to(jnp.where(live, place, -1), (8, SLOTS)).T[:, 0:1]
-    ids = lax.broadcasted_iota(jnp.int32, (SLOTS, 1), 0)
-    hit = place == lax.broadcasted_iota(jnp.int32, (SLOTS, 512), 1)
-    slot_v[...] = jnp.min(jnp.where(hit, ids, SLOTS), axis=0, keepdims=True)
+    own_basis.wait()
+    pl.semaphore_wait(barrier, len(where))
+
     to_smem = pltpu.make_async_copy(slot_v, slot_ref, slot_sem)
-    to_smem.start()
-    pl.semaphore_wait(barrier, len(where))
-
-    def densify(n, i):
-        def row(r, carry):
-            for col in range(n * 4, n * 4 + 4):
-                s = slot_ref[0, r * 32 + col]
-                xd[pl.ds(pl.multiple_of(r * BLK, BLK), BLK), col * BLK:(col + 1) * BLK] = tiles[s]
-            return carry
-        lax.fori_loop(i * 4, i * 4 + 4, row, 0)
+
+    def table():
+        b, k = coords[0:1, :], coords[1:2, :]
+        chunk = lax.shift_right_logical(b, 1)
+        dy = ((chunk & 3) - y) & 3
+        own = lax.shift_right_logical(chunk, 2) == core
+        pos = jnp.where(own, jnp.where(dy == 0, 0, jnp.where(dy == 3, 2, jnp.where(dy == 1, 3, 6))),
+                        jnp.where(dy == 0, 1, jnp.where(dy == 3, 4, jnp.where(dy == 1, 5, 7))))
+        dz = (lax.shift_right_logical(k, 2) - z) & 7
+        dz = jnp.where(dz == 0, 0, jnp.where(dz <= 3, 2 * dz - 1, jnp.where(dz == 4, 7, 2 * (NZ - dz))))
+        dx = ((k & 3) - x) & 3
+        dx = jnp.where(dx >= 2, 5 - dx, dx)
+        place = (pos * 2 + (b & 1)) * 32 + dz * NX + dx
+        live = lax.broadcasted_iota(jnp.int32, (1, SLOTS), 1) < count_ref[...]
+        place = jnp.broadcast_to(jnp.where(live, place, -1), (8, SLOTS)).T[:, 0:1]
+        ids = lax.broadcasted_iota(jnp.int32, (SLOTS, 1), 0)
+        hit = place == lax.broadcasted_iota(jnp.int32, (SLOTS, 512), 1)
+        slot_v[...] = jnp.min(jnp.where(hit, ids, SLOTS), axis=0, keepdims=True)
+        to_smem.start()
+
+    def block(rows, cols):
+        return jnp.concatenate([jnp.concatenate([tiles[slot_ref[0, r * 32 + c]] for c in range(*cols)], axis=1)
+                                for r in range(*rows)], axis=0)
 
     def loaded():
         to_smem.wait()
@@ -218,7 +218,8 @@
 
     def cells_dot(lo, hi, rows):
         right = q[lo:hi].reshape((hi - lo) * 512, RANK)
-        return jnp.dot(xd[rows, lo * 512:hi * 512], right, preferred_element_type=F32)
+        left = block((rows.start // BLK, rows.stop // BLK), (lo * 4, hi * 4))
+        return jnp.dot(left, right, preferred_element_type=F32)
 
     def cells(lo, hi, rows):
         def run():
@@ -226,20 +227,18 @@
             p[rows] = part if lo == 0 else p[rows] + part
         return run
 
-    task("load", [], 0.2, loaded, after=LOADED)
-    for n in range(NZ):
-        for i in range(4):
-            task(f"x{n}.{i}", ["load"], 0.15, lambda n=n, i=i: densify(n, i))
+    task("table", [], 0.8, table)
+    task("load", ["table"], 0.2, loaded, after=LOADED)
     for k, (lo, hi) in enumerate(GROUPS):
         came = [f"b{n}{k}{s}" for n in "xf" for s in "+-"] + (
             [f"z{n}{k}{s}" for n in "onf" for s in "+-"] if k else ["ax+", "ax-", "af+", "af-"])
         if k < 4:
             for i in range(4):
-                task(f"c{k}.{i}", [f"x{n}.{i}" for n in range(lo, hi)] + came + ([f"c{k - 1}.{i}"] if k else []), 0.35 * (hi - lo),
+                task(f"c{k}.{i}", ["load"] + came + ([f"c{k - 1}.{i}"] if k else []), 0.35 * (hi - lo),
                      cells(lo, hi, slice(i * 512, (i + 1) * 512)))
         else:
             for i in range(8):
-                task(f"c4.{i}", [f"x7.{i // 2}", f"c3.{i // 2}"] + came, 0.18, cells(lo, hi, slice(i * CHUNK, (i + 1) * CHUNK)))
+                task(f"c4.{i}", ["load", f"c3.{i // 2}"] + came, 0.18, cells(lo, hi, slice(i * CHUNK, (i + 1) * CHUNK)))
 
     def lanes(i):
         return slice(i * CHUNK, (i + 1) * CHUNK)
@@ -287,9 +286,9 @@
 
     def genes(n, i, lo, hi):
         def run():
-            cols = slice((2 * n + i) * 256, (2 * n + i + 1) * 256)
-            rows = slice(lo * CHUNK, hi * CHUNK)
-            part = jnp.dot(cbt[:, rows], xd[rows, cols], preferred_element_type=F32)
+            col = (2 * n + i) * 2
+            right = block((lo * 2, hi * 2), (col, col + 2))
+            part = jnp.dot(cbt[:, lo * CHUNK:hi * CHUNK], right, preferred_element_type=F32)
             zt[n, i] = part if lo == 0 else zt[n, i] + part
         return run
 
@@ -422,11 +421,11 @@
     return pl.pallas_call(
         kernel,
         out_shape=jax.ShapeDtypeStruct((BLK, RANK), F32),
-        in_specs=[vmem, vmem, pl.BlockSpec(memory_space=pl.ANY), vmem],
+        in_specs=[vmem, vmem, pl.BlockSpec(memory_space=pl.ANY),
+                  pl.BlockSpec(memory_space=pl.ANY)],
         out_specs=vmem,
         scratch_shapes=[
             pltpu.VMEM((SLOTS + 1, BLK, BLK), BF),
-            pltpu.VMEM((ROWS, COLS), BF),
             pltpu.VMEM((NZ, NX, BLK, RANK), BF),
             pltpu.VMEM((ROWS, RANK), F32),
             pltpu.VMEM((4, CHUNK, RANK), F32),
@@ -450,6 +449,7 @@
             pltpu.SemaphoreType.DMA((N_SEM,)),
             pltpu.SemaphoreType.DMA((8,)),
             pltpu.SemaphoreType.DMA,
+            pltpu.SemaphoreType.DMA,
         ],
         compiler_params=pltpu.CompilerParams(
             collective_id=0, has_side_effects=True, vmem_limit_bytes=60 * 1024 * 1024),

time: 81.1 us -> 80 us (0.986)
  Pallas kernels: 78.7 us -> 77.2 us
    pallas_call x1, Pallas kernels: 78.7 us -> 77.2 us  [local(): pl.pallas_call(kernel, out_shape=jax.ShapeDtypeStruct((BLK, RANK), F32),...]
where the time goes in v7:
time: 80 us; the launch traced here: 79.5 us
  Pallas kernels  77.2 us (96%)
  local copies, waits for them, and re-layouts  1.57 us (2%)
    pallas_call x1, Pallas kernels, local(): pl.pallas_call(kernel, out_shape=jax.ShapeDtypeStruct((BLK, RANK), F32),...  77.2 us

profile of v7, /device:TPU:8, one launch (start us, length us, event | category | flops | bytes accessed | tf_op | source)
XLA Modules:
  0.0 79.5 jit_solution(14939922623690825693)
XLA Ops:
  0.7 77.2 %shard_map.46 = f32[128,256]{1,0:T(8,128)} custom-call(s32[1,1]{1,0:T(1,128)S(6)} %copy.6.count_ref, s32[2,320]{1,0:T(2,128)} %bitcast.1, bf16[320,128,128]{2,1,0:T(8,128)(2,1)} %tiles_hbm.1, bf16[128,256]{1,0:T(8,128)(2,1)} %basis.1), custom_call_target="tpu_custom_call" | custom-call | flops 8589934592 | bytes 11000000 | tf_op jit(solution)/shard_map/pallas_call | solution.py:421
  77.9 1.6 %copy.7 = f32[128,256]{1,0:T(8,128)} copy(f32[128,256]{1,0:T(8,128)} %shard_map.46) | data formatting | bytes 262144

commit v8 on v7

--- a/solution.py
+++ b/solution.py
@@ -19,9 +19,9 @@
 HALF = CHUNK // 2
 SLOTS = 320
 GA = 48
-RA = 96
+RA = 64
 RB = RANK - RA
-RB1 = 80
+RB1 = 96
 
 ORDER = {0: 0, 1: 1, -1: 2, 2: 3, -2: 4, 3: 5, -3: 6, 4: 7, -4: 7}
 GROUPS = ((0, 1), (1, 3), (3, 5), (5, 7), (7, 8))

time: 80 us -> 80.8 us (1.010)
  Pallas kernels: 77.2 us -> 78.5 us
    pallas_call x1, Pallas kernels: 77.2 us -> 78.5 us  [local(): pl.pallas_call(kernel, out_shape=jax.ShapeDtypeStruct((BLK, RANK), F32),...]
where the time goes in v8:
time: 80.8 us; the launch traced here: 80.7 us
  Pallas kernels  78.5 us (97%)
  local copies, waits for them, and re-layouts  1.57 us (2%)
    pallas_call x1, Pallas kernels, local(): pl.pallas_call(kernel, out_shape=jax.ShapeDtypeStruct((BLK, RANK), F32),...  78.5 us

profile of v8, /device:TPU:8, one launch (start us, length us, event | category | flops | bytes accessed | tf_op | source)
XLA Modules:
  0.0 80.7 jit_solution(11403892311095013443)
XLA Ops:
  0.7 78.5 %shard_map.46 = f32[128,256]{1,0:T(8,128)} custom-call(s32[1,1]{1,0:T(1,128)S(6)} %copy.6.count_ref, s32[2,320]{1,0:T(2,128)} %bitcast.1, bf16[320,128,128]{2,1,0:T(8,128)(2,1)} %tiles_hbm.1, bf16[128,256]{1,0:T(8,128)(2,1)} %basis.1), custom_call_target="tpu_custom_call" | custom-call | flops 8589934592 | bytes 11000000 | tf_op jit(solution)/shard_map/pallas_call | solution.py:421
  79.1 1.6 %copy.7 = f32[128,256]{1,0:T(8,128)} copy(f32[128,256]{1,0:T(8,128)} %shard_map.46) | data formatting | bytes 262144

commit v9 on v8

--- a/solution.py
+++ b/solution.py
@@ -125,7 +125,7 @@
                 self.tasks[name][3][0].wait_send()
 
 
-def kernel(count_ref, coords, tiles_hbm, basis, out, tiles, q, p, pcr, ys, yr, cbt, zt,
+def kernel(count_ref, coords, tiles_hbm, basis, out, tiles, q, p, pcs, pcr, ys, yr, cbt, zt,
            za, zb, azs, azr, axr, axr2, bs, br, bzs, bzr, slot_v, slot_ref, ssem, rsem, tsem, slot_sem, basis_sem):
     c = lax.axis_index("cells")
     g = lax.axis_index("genes")
@@ -243,17 +243,18 @@
     def lanes(i):
         return slice(i * CHUNK, (i + 1) * CHUNK)
 
-    def add(rows, other):
-        def run():
-            p[rows] = p[rows] + other[...]
-        return run
-
     OWN, OTHER = {0: 0, -1: 2, 1: 3, 2: 6}, {0: 1, -1: 4, 1: 5, 2: 7}
     low = {dy: slice(i * CHUNK, i * CHUNK + HALF) for dy, i in OWN.items()}
     high = {dy: slice(i * CHUNK + HALF, (i + 1) * CHUNK) for dy, i in OWN.items()}
     for dy in (2, 1, -1, 0):
-        send(f"pair{dy}", [f"c4.{OTHER[dy]}"], p.at[lanes(OTHER[dy])], pcr.at[dy + 1], "c")
-        task(f"own{dy}", [f"c4.{OWN[dy]}", f"pair{dy}"], 0.1, add(lanes(OWN[dy]), pcr.at[dy + 1]))
+        def to_other(dy=dy):
+            pcs[dy + 1] = pack(p[lanes(OTHER[dy])])
+
+        def from_other(dy=dy):
+            p[lanes(OWN[dy])] = p[lanes(OWN[dy])] + unpack(pcr[dy + 1])
+
+        send(f"pair{dy}", [f"c4.{OTHER[dy]}"], pcs.at[dy + 1], pcr.at[dy + 1], "c", to_other, 0.25)
+        task(f"own{dy}", [f"c4.{OWN[dy]}", f"pair{dy}"], 0.15, from_other)
 
     def y_send(n, needs, rows, to, first=None):
         def run():
@@ -428,7 +429,8 @@
             pltpu.VMEM((SLOTS + 1, BLK, BLK), BF),
             pltpu.VMEM((NZ, NX, BLK, RANK), BF),
             pltpu.VMEM((ROWS, RANK), F32),
-            pltpu.VMEM((4, CHUNK, RANK), F32),
+            pltpu.VMEM((4, CHUNK + HEAD, RANK), jnp.int16),
+            pltpu.VMEM((4, CHUNK + HEAD, RANK), jnp.int16),
             pltpu.VMEM((6, HALF + HEAD, RANK), jnp.int16),
             pltpu.VMEM((6, HALF + HEAD, RANK), jnp.int16),
             pltpu.VMEM((RANK, ROWS), BF),

time: 80.8 us -> 79.6 us (0.985)
  Pallas kernels: 78.5 us -> 77.2 us
    pallas_call x1, Pallas kernels: 78.5 us -> 77.2 us  [local(): pl.pallas_call(kernel, out_shape=jax.ShapeDtypeStruct((BLK, RANK), F32),...]
where the time goes in v9:
time: 79.6 us; the launch traced here: 79.5 us
  Pallas kernels  77.2 us (97%)
  local copies, waits for them, and re-layouts  1.57 us (2%)
    pallas_call x1, Pallas kernels, local(): pl.pallas_call(kernel, out_shape=jax.ShapeDtypeStruct((BLK, RANK), F32),...  77.2 us

profile of v9, /device:TPU:8, one launch (start us, length us, event | category | flops | bytes accessed | tf_op | source)
XLA Modules:
  0.0 79.5 jit_solution(3881613796573277331)
XLA Ops:
  0.7 77.2 %shard_map.46 = f32[128,256]{1,0:T(8,128)} custom-call(s32[1,1]{1,0:T(1,128)S(6)} %copy.6.count_ref, s32[2,320]{1,0:T(2,128)} %bitcast.1, bf16[320,128,128]{2,1,0:T(8,128)(2,1)} %tiles_hbm.1, bf16[128,256]{1,0:T(8,128)(2,1)} %basis.1), custom_call_target="tpu_custom_call" | custom-call | flops 8589934592 | bytes 11000000 | tf_op jit(solution)/shard_map/pallas_call | solution.py:422
  77.9 1.6 %copy.7 = f32[128,256]{1,0:T(8,128)} copy(f32[128,256]{1,0:T(8,128)} %shard_map.46) | data formatting | bytes 262144
